TPU v7x, 32 devices: a whole 2x2x4 slice. The times are simulated.
32 devices in a mesh: segment: 8 (over y, x, core), band: 4 (over z).
Axes of the slice: x: 2, y: 2, z: 4, core: 2. Of those that a mesh axis runs over, the one named last changes fastest.
Arguments:
- pixels: bfloat16 [2, 16, 16, 256], P(None, 'band'), may hold values from -6 to 6
- conv_weight: bfloat16 [8, 4, 3, 3, 256, 256], P('segment'), may hold values from -0.1875 to 0.1875
- join_weight: bfloat16 [8, 256, 256], P('segment'), may hold values from -0.25 to 0.25
Outputs:
- decoded: bfloat16 [2, 16, 16, 256], P(None, 'band', 'segment')
All inputs are finite; a program needn't handle non-finite values.
Results may differ from a plain program's by a relative error of at most 0.024.
Values may be sent and summed in bfloat16 or wider, within the bound.
A program may use at most 64 MiB of HBM per device.

v0:
```python
import jax
import jax.numpy as jnp
from jax import lax
from jax.sharding import PartitionSpec as P


def partner(shard, axis, stride):
    return lax.ppermute(shard, axis, [(i, i ^ 1 << stride) for i in range(lax.axis_size(axis))])


def padded(block, sides, width):
    for axis, dim in sides:
        count = lax.axis_size(axis)
        forward = [(i, i + 1) for i in range(count - 1)]
        backward = [(target, source) for source, target in forward]
        low = lax.ppermute(
            lax.slice_in_dim(block, block.shape[dim] - width, None, axis=dim), axis, forward
        )
        high = lax.ppermute(lax.slice_in_dim(block, 0, width, axis=dim), axis, backward)
        block = jnp.concatenate([low, block, high], axis=dim)
    return block


def shifted(value, axis, steps):
    count = lax.axis_size(axis)
    leading, last = (max(0, -steps), min(count, count - steps))
    return lax.ppermute(value, axis, [(source, source + steps) for source in range(leading, last)])


def normed(hidden):
    values = hidden.astype(jnp.float32)
    scale = lax.rsqrt(jnp.mean(values * values, axis=-1, keepdims=True) + 1e-05)
    return (values * scale).astype(jnp.bfloat16)


def conv_rows(extended, kernel):
    result = lax.conv_general_dilated(
        extended[None],
        kernel,
        (1, 1),
        ((0, 0), (1, 1)),
        dimension_numbers=("NHWC", "HWIO", "NHWC"),
        preferred_element_type=jnp.float32,
    )[0]
    return jnp.maximum(result, 0.0)


def shards(pixels, conv_weight, join_weight):
    segments = lax.axis_size("segment")
    halfway = segments // 2
    bit_count = segments.bit_length() - 1
    band_count = lax.axis_size("band")
    segment_at = lax.axis_index("segment")
    band_at = lax.axis_index("band")
    batches, height, columns, channels = pixels.shape
    layers = conv_weight[0]
    conv_count = layers.shape[0]
    own_join = join_weight[0]
    mirror_join = own_join
    for bit_pos in range(bit_count):
        mirror_join = partner(mirror_join, "segment", bit_pos)
    decoding = segment_at >= halfway
    is_final = segment_at == segments - 1

    def section(hidden):
        extended = padded(hidden, (("band", 0),), conv_count)
        for layer in range(conv_count):
            active_part = conv_rows(normed(extended), layers[layer])
            extended = (extended[1:-1].astype(jnp.float32) + active_part).astype(jnp.bfloat16)
            margin = conv_count - 1 - layer
            if margin > 0:
                global_row = (
                    band_at * height - margin + jnp.arange(height + 2 * margin, dtype=jnp.int32)
                )
                inside = (global_row >= 0) & (global_row < height * band_count)
                extended = jnp.where(inside[:, None, None], extended, jnp.zeros_like(extended))
        return extended

    def run_tick(tick_at, carried):
        incoming, skip_store, out_store = carried
        opening = lax.dynamic_index_in_dim(
            pixels, jnp.minimum(tick_at, batches - 1), 0, keepdims=False
        )
        source = jnp.where(segment_at == 0, opening, incoming)
        slot_at = jnp.clip(tick_at - segment_at, 0, batches - 1)
        skipped = lax.dynamic_index_in_dim(skip_store, slot_at, 0, keepdims=False)
        joining = (
            jnp.dot(skipped, mirror_join, preferred_element_type=jnp.float32)
            + jnp.dot(source, own_join, preferred_element_type=jnp.float32)
        ).astype(jnp.bfloat16)
        hidden = section(jnp.where(decoding, joining, source))
        active = (tick_at - segment_at >= 0) & (tick_at - segment_at < batches)
        previous = lax.dynamic_index_in_dim(out_store, slot_at, 0, keepdims=False)
        out_store = lax.dynamic_update_index_in_dim(
            out_store, jnp.where(active & is_final, normed(hidden), previous), slot_at, 0
        )
        mirrored = hidden
        for bit_pos in range(bit_count):
            mirrored = partner(mirrored, "segment", bit_pos)
        anchor = tick_at - (segments - 1 - segment_at)
        wanted = decoding & (anchor >= 0) & (anchor < batches)
        target = jnp.clip(anchor, 0, batches - 1)
        stored = lax.dynamic_index_in_dim(skip_store, target, 0, keepdims=False)
        skip_store = lax.dynamic_update_index_in_dim(
            skip_store, jnp.where(wanted, mirrored, stored), target, 0
        )
        incoming = shifted(hidden, "segment", 1)
        return (incoming, skip_store, out_store)

    def with_skips(tick_at, carried):
        return run_tick(tick_at, carried)

    blank = jnp.zeros((height, columns, channels), jnp.bfloat16)
    stacked = jnp.zeros((batches, height, columns, channels), jnp.bfloat16)
    carried = (blank, stacked, stacked)
    tick_total = batches + segments - 1
    carried = lax.fori_loop(0, tick_total, with_skips, carried)
    spread = lax.all_to_all(carried[2], "segment", split_axis=2, concat_axis=0, tiled=True)
    return spread[(segments - 1) * batches :]


def solution(mesh):
    return jax.shard_map(
        shards,
        mesh=mesh,
        in_specs=(
            P(None, "band", None, None),
            P("segment", None, None, None, None, None),
            P("segment", None, None),
        ),
        out_specs=P(None, "band", "segment", None),
        check_vma=False,
    )
```

profile of v0, /device:TPU:0, one launch (start us, length us, event | category | flops | bytes accessed | tf_op | source)
XLA Modules:
  0.0 278.3 jit_solution(9652790032256149703)
XLA Ops:
  1.7 2.8 %collective-permute-start.7 = (bf16[256,256]{1,0:T(8,128)(2,1)S(1)}, bf16[256,256]{1,0:T(8,128)(2,1)S(1)}, u32[]{:S(2)}, u32[]{:S(2)}) collective-permute-start(bf16[256,256]{1,0:T(8,128)(2,1)S(1)} %collective-permute-done.6), channel_id=1, source_target_pairs={{0,8},{4,12},{8,0},{12,4},{16,24},{20,28},{24,16},{28,20},{1,9},{5... | collective-permute-start | bytes 393224 | tf_op jit(solution)/shard_map/ppermute | solution.py:8
  4.5 3.8 %collective-permute-done.7 = bf16[256,256]{1,0:T(8,128)(2,1)S(1)} collective-permute-done((bf16[256,256]{1,0:T(8,128)(2,1)S(1)}, bf16[256,256]{1,0:T(8,128)(2,1)S(1)}, u32[]{:S(2)}, u32[]{:S(2)}) %collective-permute-start.7) | collective-permute-done | bytes 131104 | tf_op jit(solution)/shard_map/ppermute | solution.py:8
  10.1 3.3 %collective-permute-done.8 = bf16[256,256]{1,0:T(8,128)(2,1)S(1)} collective-permute-done((bf16[256,256]{1,0:T(8,128)(2,1)S(1)}, bf16[256,256]{1,0:T(8,128)(2,1)S(1)}, u32[]{:S(2)}, u32[]{:S(2)}) %collective-permute-start.8) | collective-permute-done | bytes 131104 | tf_op jit(solution)/shard_map/ppermute | solution.py:8
  13.4 256.8 %while.19 = (s32[]{:T(128)}, bf16[4,16,256]{2,1,0:T(8,128)(2,1)S(1)}, bf16[2,4,16,256]{3,2,1,0:T(8,128)(2,1)S(1)}, bf16[2,4,16,256]{3,1,0,2:T(4,128)(2,1)S(1)}, ...) while((s32[]{:T(128)}, ...), condition=%wide.region_6.7_spmd, body=%wide.region_0.6_spmd.sunk | while | flops 813793920 | bytes 15107953 | solution.py:117
  16.0 4.5 %collective-permute-start.1 = (bf16[4,16,256]{2,1,0:T(8,128)(2,1)S(1)}, bf16[4,16,256]{2,1,0:T(8,128)(2,1)S(1)}, u32[]{:S(2)}, u32[]{:S(2)}) collective-permute-start(bf16[4,16,256]{2,1,0:T(8,128)(2,1)S(1)} %fusion.158), channel_id=1, source_target_pairs={{0,1},{1,2},{2,3},{4,5},{5,6},{6,7},{8,9},{9,10},{10,11},{12,13},{... | collective-permute-start | bytes 98312 | tf_op jit(solution)/shard_map/while/body/eval_jaxpr/ppermute | solution.py:16
  35.4 2.5 collective-permute-done.4
  44.4 4.8 %collective-permute-start.1 = (bf16[4,16,256]{2,1,0:T(8,128)(2,1)S(1)}, bf16[4,16,256]{2,1,0:T(8,128)(2,1)S(1)}, u32[]{:S(2)}, u32[]{:S(2)}) collective-permute-start(bf16[4,16,256]{2,1,0:T(8,128)(2,1)S(1)} %fusion.158), channel_id=1, source_target_pairs={{0,1},{1,2},{2,3},{4,5},{5,6},{6,7},{8,9},{9,10},{10,11},{12,13},{... | collective-permute-start | bytes 98312 | tf_op jit(solution)/shard_map/while/body/eval_jaxpr/ppermute | solution.py:16
  63.9 2.7 collective-permute-done.4
  73.1 4.9 %collective-permute-start.1 = (bf16[4,16,256]{2,1,0:T(8,128)(2,1)S(1)}, bf16[4,16,256]{2,1,0:T(8,128)(2,1)S(1)}, u32[]{:S(2)}, u32[]{:S(2)}) collective-permute-start(bf16[4,16,256]{2,1,0:T(8,128)(2,1)S(1)} %fusion.158), channel_id=1, source_target_pairs={{0,1},{1,2},{2,3},{4,5},{5,6},{6,7},{8,9},{9,10},{10,11},{12,13},{... | collective-permute-start | bytes 98312 | tf_op jit(solution)/shard_map/while/body/eval_jaxpr/ppermute | solution.py:16
  88.6 2.4 collective-permute-start.2
  92.5 2.8 %collective-permute-done.4 = bf16[4,16,256]{2,1,0:T(8,128)(2,1)S(1)} collective-permute-done((bf16[4,16,256]{2,1,0:T(8,128)(2,1)S(1)}, bf16[4,16,256]{2,1,0:T(8,128)(2,1)S(1)}, u32[]{:S(2)}, u32[]{:S(2)}) %collective-permute-start.4) | collective-permute-done | bytes 32800 | tf_op jit(solution)/shard_map/while/body/eval_jaxpr/ppermute | solution.py:8
  96.5 2.7 collective-permute-done.5
  101.8 4.9 %collective-permute-start.1 = (bf16[4,16,256]{2,1,0:T(8,128)(2,1)S(1)}, bf16[4,16,256]{2,1,0:T(8,128)(2,1)S(1)}, u32[]{:S(2)}, u32[]{:S(2)}) collective-permute-start(bf16[4,16,256]{2,1,0:T(8,128)(2,1)S(1)} %fusion.158), channel_id=1, source_target_pairs={{0,1},{1,2},{2,3},{4,5},{5,6},{6,7},{8,9},{9,10},{10,11},{12,13},{... | collective-permute-start | bytes 98312 | tf_op jit(solution)/shard_map/while/body/eval_jaxpr/ppermute | solution.py:16
  117.3 2.4 collective-permute-start.2
  121.0 2.8 %collective-permute-done.4 = bf16[4,16,256]{2,1,0:T(8,128)(2,1)S(1)} collective-permute-done((bf16[4,16,256]{2,1,0:T(8,128)(2,1)S(1)}, bf16[4,16,256]{2,1,0:T(8,128)(2,1)S(1)}, u32[]{:S(2)}, u32[]{:S(2)}) %collective-permute-start.4) | collective-permute-done | bytes 32800 | tf_op jit(solution)/shard_map/while/body/eval_jaxpr/ppermute | solution.py:8
  124.9 2.9 %collective-permute-done.5 = bf16[4,16,256]{2,1,0:T(8,128)(2,1)S(1)} collective-permute-done((bf16[4,16,256]{2,1,0:T(8,128)(2,1)S(1)}, bf16[4,16,256]{2,1,0:T(8,128)(2,1)S(1)}, u32[]{:S(2)}, u32[]{:S(2)}) %collective-permute-start.5) | collective-permute-done | bytes 32800 | tf_op jit(solution)/shard_map/while/body/eval_jaxpr/ppermute | solution.py:8
  130.4 4.9 %collective-permute-start.1 = (bf16[4,16,256]{2,1,0:T(8,128)(2,1)S(1)}, bf16[4,16,256]{2,1,0:T(8,128)(2,1)S(1)}, u32[]{:S(2)}, u32[]{:S(2)}) collective-permute-start(bf16[4,16,256]{2,1,0:T(8,128)(2,1)S(1)} %fusion.158), channel_id=1, source_target_pairs={{0,1},{1,2},{2,3},{4,5},{5,6},{6,7},{8,9},{9,10},{10,11},{12,13},{... | collective-permute-start | bytes 98312 | tf_op jit(solution)/shard_map/while/body/eval_jaxpr/ppermute | solution.py:16
  149.6 2.8 %collective-permute-done.4 = bf16[4,16,256]{2,1,0:T(8,128)(2,1)S(1)} collective-permute-done((bf16[4,16,256]{2,1,0:T(8,128)(2,1)S(1)}, bf16[4,16,256]{2,1,0:T(8,128)(2,1)S(1)}, u32[]{:S(2)}, u32[]{:S(2)}) %collective-permute-start.4) | collective-permute-done | bytes 32800 | tf_op jit(solution)/shard_map/while/body/eval_jaxpr/ppermute | solution.py:8
  153.3 3.0 %collective-permute-done.5 = bf16[4,16,256]{2,1,0:T(8,128)(2,1)S(1)} collective-permute-done((bf16[4,16,256]{2,1,0:T(8,128)(2,1)S(1)}, bf16[4,16,256]{2,1,0:T(8,128)(2,1)S(1)}, u32[]{:S(2)}, u32[]{:S(2)}) %collective-permute-start.5) | collective-permute-done | bytes 32800 | tf_op jit(solution)/shard_map/while/body/eval_jaxpr/ppermute | solution.py:8
  158.9 4.8 %collective-permute-start.1 = (bf16[4,16,256]{2,1,0:T(8,128)(2,1)S(1)}, bf16[4,16,256]{2,1,0:T(8,128)(2,1)S(1)}, u32[]{:S(2)}, u32[]{:S(2)}) collective-permute-start(bf16[4,16,256]{2,1,0:T(8,128)(2,1)S(1)} %fusion.158), channel_id=1, source_target_pairs={{0,1},{1,2},{2,3},{4,5},{5,6},{6,7},{8,9},{9,10},{10,11},{12,13},{... | collective-permute-start | bytes 98312 | tf_op jit(solution)/shard_map/while/body/eval_jaxpr/ppermute | solution.py:16
  178.3 2.8 %collective-permute-done.4 = bf16[4,16,256]{2,1,0:T(8,128)(2,1)S(1)} collective-permute-done((bf16[4,16,256]{2,1,0:T(8,128)(2,1)S(1)}, bf16[4,16,256]{2,1,0:T(8,128)(2,1)S(1)}, u32[]{:S(2)}, u32[]{:S(2)}) %collective-permute-start.4) | collective-permute-done | bytes 32800 | tf_op jit(solution)/shard_map/while/body/eval_jaxpr/ppermute | solution.py:8
  181.7 3.4 %collective-permute-done.5 = bf16[4,16,256]{2,1,0:T(8,128)(2,1)S(1)} collective-permute-done((bf16[4,16,256]{2,1,0:T(8,128)(2,1)S(1)}, bf16[4,16,256]{2,1,0:T(8,128)(2,1)S(1)}, u32[]{:S(2)}, u32[]{:S(2)}) %collective-permute-start.5) | collective-permute-done | bytes 32800 | tf_op jit(solution)/shard_map/while/body/eval_jaxpr/ppermute | solution.py:8
  187.6 4.9 %collective-permute-start.1 = (bf16[4,16,256]{2,1,0:T(8,128)(2,1)S(1)}, bf16[4,16,256]{2,1,0:T(8,128)(2,1)S(1)}, u32[]{:S(2)}, u32[]{:S(2)}) collective-permute-start(bf16[4,16,256]{2,1,0:T(8,128)(2,1)S(1)} %fusion.158), channel_id=1, source_target_pairs={{0,1},{1,2},{2,3},{4,5},{5,6},{6,7},{8,9},{9,10},{10,11},{12,13},{... | collective-permute-start | bytes 98312 | tf_op jit(solution)/shard_map/while/body/eval_jaxpr/ppermute | solution.py:16
  206.7 2.8 %collective-permute-done.4 = bf16[4,16,256]{2,1,0:T(8,128)(2,1)S(1)} collective-permute-done((bf16[4,16,256]{2,1,0:T(8,128)(2,1)S(1)}, bf16[4,16,256]{2,1,0:T(8,128)(2,1)S(1)}, u32[]{:S(2)}, u32[]{:S(2)}) %collective-permute-start.4) | collective-permute-done | bytes 32800 | tf_op jit(solution)/shard_map/while/body/eval_jaxpr/ppermute | solution.py:8
  210.1 3.4 %collective-permute-done.5 = bf16[4,16,256]{2,1,0:T(8,128)(2,1)S(1)} collective-permute-done((bf16[4,16,256]{2,1,0:T(8,128)(2,1)S(1)}, bf16[4,16,256]{2,1,0:T(8,128)(2,1)S(1)}, u32[]{:S(2)}, u32[]{:S(2)}) %collective-permute-start.5) | collective-permute-done | bytes 32800 | tf_op jit(solution)/shard_map/while/body/eval_jaxpr/ppermute | solution.py:8
  216.0 4.8 %collective-permute-start.1 = (bf16[4,16,256]{2,1,0:T(8,128)(2,1)S(1)}, bf16[4,16,256]{2,1,0:T(8,128)(2,1)S(1)}, u32[]{:S(2)}, u32[]{:S(2)}) collective-permute-start(bf16[4,16,256]{2,1,0:T(8,128)(2,1)S(1)} %fusion.158), channel_id=1, source_target_pairs={{0,1},{1,2},{2,3},{4,5},{5,6},{6,7},{8,9},{9,10},{10,11},{12,13},{... | collective-permute-start | bytes 98312 | tf_op jit(solution)/shard_map/while/body/eval_jaxpr/ppermute | solution.py:16
  235.0 2.8 %collective-permute-done.4 = bf16[4,16,256]{2,1,0:T(8,128)(2,1)S(1)} collective-permute-done((bf16[4,16,256]{2,1,0:T(8,128)(2,1)S(1)}, bf16[4,16,256]{2,1,0:T(8,128)(2,1)S(1)}, u32[]{:S(2)}, u32[]{:S(2)}) %collective-permute-start.4) | collective-permute-done | bytes 32800 | tf_op jit(solution)/shard_map/while/body/eval_jaxpr/ppermute | solution.py:8
  238.4 3.4 %collective-permute-done.5 = bf16[4,16,256]{2,1,0:T(8,128)(2,1)S(1)} collective-permute-done((bf16[4,16,256]{2,1,0:T(8,128)(2,1)S(1)}, bf16[4,16,256]{2,1,0:T(8,128)(2,1)S(1)}, u32[]{:S(2)}, u32[]{:S(2)}) %collective-permute-start.5) | collective-permute-done | bytes 32800 | tf_op jit(solution)/shard_map/while/body/eval_jaxpr/ppermute | solution.py:8
  244.4 4.8 %collective-permute-start.1 = (bf16[4,16,256]{2,1,0:T(8,128)(2,1)S(1)}, bf16[4,16,256]{2,1,0:T(8,128)(2,1)S(1)}, u32[]{:S(2)}, u32[]{:S(2)}) collective-permute-start(bf16[4,16,256]{2,1,0:T(8,128)(2,1)S(1)} %fusion.158), channel_id=1, source_target_pairs={{0,1},{1,2},{2,3},{4,5},{5,6},{6,7},{8,9},{9,10},{10,11},{12,13},{... | collective-permute-start | bytes 98312 | tf_op jit(solution)/shard_map/while/body/eval_jaxpr/ppermute | solution.py:16
  263.4 2.8 %collective-permute-done.4 = bf16[4,16,256]{2,1,0:T(8,128)(2,1)S(1)} collective-permute-done((bf16[4,16,256]{2,1,0:T(8,128)(2,1)S(1)}, bf16[4,16,256]{2,1,0:T(8,128)(2,1)S(1)}, u32[]{:S(2)}, u32[]{:S(2)}) %collective-permute-start.4) | collective-permute-done | bytes 32800 | tf_op jit(solution)/shard_map/while/body/eval_jaxpr/ppermute | solution.py:8
  266.8 3.4 %collective-permute-done.5 = bf16[4,16,256]{2,1,0:T(8,128)(2,1)S(1)} collective-permute-done((bf16[4,16,256]{2,1,0:T(8,128)(2,1)S(1)}, bf16[4,16,256]{2,1,0:T(8,128)(2,1)S(1)}, u32[]{:S(2)}, u32[]{:S(2)}) %collective-permute-start.5) | collective-permute-done | bytes 32800 | tf_op jit(solution)/shard_map/while/body/eval_jaxpr/ppermute | solution.py:8
  270.2 7.4 %all_to_all.15 = bf16[2,4,16,256]{3,1,0,2:T(4,128)(2,1)S(1)} all-to-all(bf16[2,4,16,256]{3,1,0,2:T(4,128)(2,1)S(1)} %get-tuple-element.305), channel_id=1, replica_groups=mesh['segment'=8,'band'=4] {'segment'}, dimensions={2} | all-to-all | bytes 131072 | tf_op jit(solution)/shard_map/all_to_all | solution.py:118
  (576 shorter events, 161.3 us)
Async XLA Ops:
  1.7 6.7 %collective-permute-start.7 = (bf16[256,256]{1,0:T(8,128)(2,1)S(1)}, bf16[256,256]{1,0:T(8,128)(2,1)S(1)}, u32[]{:S(2)}, u32[]{:S(2)}) collective-permute-start(bf16[256,256]{1,0:T(8,128)(2,1)S(1)} %collective-permute-done.6), channel_id=1, source_target_pairs={{0,8},{4,12},{8,0},{12,4},{16,24},{20,28},{24,16},{28,20},{1,9},{5... | collective-permute-start | bytes 393224 | tf_op jit(solution)/shard_map/ppermute | solution.py:8
  8.3 5.0 %collective-permute-start.8 = (bf16[256,256]{1,0:T(8,128)(2,1)S(1)}, bf16[256,256]{1,0:T(8,128)(2,1)S(1)}, u32[]{:S(2)}, u32[]{:S(2)}) collective-permute-start(bf16[256,256]{1,0:T(8,128)(2,1)S(1)} %collective-permute-done.7), channel_id=1, source_target_pairs={{0,16},{4,20},{8,24},{12,28},{16,0},{20,4},{24,8},{28,12},{1,17},{... | collective-permute-start | bytes 393224 | tf_op jit(solution)/shard_map/ppermute | solution.py:8
  14.7 6.0 %collective-permute-start = (bf16[4,16,256]{2,1,0:T(8,128)(2,1)S(1)}, bf16[4,16,256]{2,1,0:T(8,128)(2,1)S(1)}, u32[]{:S(2)}, u32[]{:S(2)}) collective-permute-start(bf16[4,16,256]{2,1,0:T(8,128)(2,1)S(1)} %fusion.158), channel_id=1, source_target_pairs={{1,0},{2,1},{3,2},{5,4},{6,5},{7,6},{9,8},{10,9},{11,10},{13,12},{... | collective-permute-start | bytes 98312 | tf_op jit(solution)/shard_map/while/body/eval_jaxpr/ppermute | solution.py:19
  16.0 6.1 %collective-permute-start.1 = (bf16[4,16,256]{2,1,0:T(8,128)(2,1)S(1)}, bf16[4,16,256]{2,1,0:T(8,128)(2,1)S(1)}, u32[]{:S(2)}, u32[]{:S(2)}) collective-permute-start(bf16[4,16,256]{2,1,0:T(8,128)(2,1)S(1)} %fusion.158), channel_id=1, source_target_pairs={{0,1},{1,2},{2,3},{4,5},{5,6},{6,7},{8,9},{9,10},{10,11},{12,13},{... | collective-permute-start | bytes 98312 | tf_op jit(solution)/shard_map/while/body/eval_jaxpr/ppermute | solution.py:16
  31.1 10.7 %collective-permute-start.2 = (bf16[4,16,256]{2,1,0:T(8,128)(2,1)S(1)}, bf16[4,16,256]{2,1,0:T(8,128)(2,1)S(1)}, u32[]{:S(2)}, u32[]{:S(2)}) collective-permute-start(bf16[4,16,256]{2,1,0:T(8,128)(2,1)S(1)} %get-tuple-element.463), channel_id=1, source_target_pairs={{0,4},{4,8},{8,12},{12,16},{16,20},{20,24},{24,28},{1,5},{5,9},{9,... | collective-permute-start | bytes 98312 | tf_op jit(solution)/shard_map/while/body/eval_jaxpr/ppermute | solution.py:27
  33.5 4.3 %collective-permute-start.4 = (bf16[4,16,256]{2,1,0:T(8,128)(2,1)S(1)}, bf16[4,16,256]{2,1,0:T(8,128)(2,1)S(1)}, u32[]{:S(2)}, u32[]{:S(2)}) collective-permute-start(bf16[4,16,256]{2,1,0:T(8,128)(2,1)S(1)} %collective-permute-done.3), channel_id=1, source_target_pairs={{0,8},{4,12},{8,0},{12,4},{16,24},{20,28},{24,16},{28,20},{1,9},{5... | collective-permute-start | bytes 98312 | tf_op jit(solution)/shard_map/while/body/eval_jaxpr/ppermute | solution.py:8
  43.1 6.3 %collective-permute-start = (bf16[4,16,256]{2,1,0:T(8,128)(2,1)S(1)}, bf16[4,16,256]{2,1,0:T(8,128)(2,1)S(1)}, u32[]{:S(2)}, u32[]{:S(2)}) collective-permute-start(bf16[4,16,256]{2,1,0:T(8,128)(2,1)S(1)} %fusion.158), channel_id=1, source_target_pairs={{1,0},{2,1},{3,2},{5,4},{6,5},{7,6},{9,8},{10,9},{11,10},{13,12},{... | collective-permute-start | bytes 98312 | tf_op jit(solution)/shard_map/while/body/eval_jaxpr/ppermute | solution.py:19
  44.4 6.4 %collective-permute-start.1 = (bf16[4,16,256]{2,1,0:T(8,128)(2,1)S(1)}, bf16[4,16,256]{2,1,0:T(8,128)(2,1)S(1)}, u32[]{:S(2)}, u32[]{:S(2)}) collective-permute-start(bf16[4,16,256]{2,1,0:T(8,128)(2,1)S(1)} %fusion.158), channel_id=1, source_target_pairs={{0,1},{1,2},{2,3},{4,5},{5,6},{6,7},{8,9},{9,10},{10,11},{12,13},{... | collective-permute-start | bytes 98312 | tf_op jit(solution)/shard_map/while/body/eval_jaxpr/ppermute | solution.py:16
  59.8 10.7 %collective-permute-start.2 = (bf16[4,16,256]{2,1,0:T(8,128)(2,1)S(1)}, bf16[4,16,256]{2,1,0:T(8,128)(2,1)S(1)}, u32[]{:S(2)}, u32[]{:S(2)}) collective-permute-start(bf16[4,16,256]{2,1,0:T(8,128)(2,1)S(1)} %get-tuple-element.463), channel_id=1, source_target_pairs={{0,4},{4,8},{8,12},{12,16},{16,20},{20,24},{24,28},{1,5},{5,9},{9,... | collective-permute-start | bytes 98312 | tf_op jit(solution)/shard_map/while/body/eval_jaxpr/ppermute | solution.py:27
  62.3 4.3 %collective-permute-start.4 = (bf16[4,16,256]{2,1,0:T(8,128)(2,1)S(1)}, bf16[4,16,256]{2,1,0:T(8,128)(2,1)S(1)}, u32[]{:S(2)}, u32[]{:S(2)}) collective-permute-start(bf16[4,16,256]{2,1,0:T(8,128)(2,1)S(1)} %collective-permute-done.3), channel_id=1, source_target_pairs={{0,8},{4,12},{8,0},{12,4},{16,24},{20,28},{24,16},{28,20},{1,9},{5... | collective-permute-start | bytes 98312 | tf_op jit(solution)/shard_map/while/body/eval_jaxpr/ppermute | solution.py:8
  71.8 6.3 %collective-permute-start = (bf16[4,16,256]{2,1,0:T(8,128)(2,1)S(1)}, bf16[4,16,256]{2,1,0:T(8,128)(2,1)S(1)}, u32[]{:S(2)}, u32[]{:S(2)}) collective-permute-start(bf16[4,16,256]{2,1,0:T(8,128)(2,1)S(1)} %fusion.158), channel_id=1, source_target_pairs={{1,0},{2,1},{3,2},{5,4},{6,5},{7,6},{9,8},{10,9},{11,10},{13,12},{... | collective-permute-start | bytes 98312 | tf_op jit(solution)/shard_map/while/body/eval_jaxpr/ppermute | solution.py:19
  73.1 6.4 %collective-permute-start.1 = (bf16[4,16,256]{2,1,0:T(8,128)(2,1)S(1)}, bf16[4,16,256]{2,1,0:T(8,128)(2,1)S(1)}, u32[]{:S(2)}, u32[]{:S(2)}) collective-permute-start(bf16[4,16,256]{2,1,0:T(8,128)(2,1)S(1)} %fusion.158), channel_id=1, source_target_pairs={{0,1},{1,2},{2,3},{4,5},{5,6},{6,7},{8,9},{9,10},{10,11},{12,13},{... | collective-permute-start | bytes 98312 | tf_op jit(solution)/shard_map/while/body/eval_jaxpr/ppermute | solution.py:16
  88.6 10.7 %collective-permute-start.2 = (bf16[4,16,256]{2,1,0:T(8,128)(2,1)S(1)}, bf16[4,16,256]{2,1,0:T(8,128)(2,1)S(1)}, u32[]{:S(2)}, u32[]{:S(2)}) collective-permute-start(bf16[4,16,256]{2,1,0:T(8,128)(2,1)S(1)} %get-tuple-element.463), channel_id=1, source_target_pairs={{0,4},{4,8},{8,12},{12,16},{16,20},{20,24},{24,28},{1,5},{5,9},{9,... | collective-permute-start | bytes 98312 | tf_op jit(solution)/shard_map/while/body/eval_jaxpr/ppermute | solution.py:27
  91.0 4.3 %collective-permute-start.4 = (bf16[4,16,256]{2,1,0:T(8,128)(2,1)S(1)}, bf16[4,16,256]{2,1,0:T(8,128)(2,1)S(1)}, u32[]{:S(2)}, u32[]{:S(2)}) collective-permute-start(bf16[4,16,256]{2,1,0:T(8,128)(2,1)S(1)} %collective-permute-done.3), channel_id=1, source_target_pairs={{0,8},{4,12},{8,0},{12,4},{16,24},{20,28},{24,16},{28,20},{1,9},{5... | collective-permute-start | bytes 98312 | tf_op jit(solution)/shard_map/while/body/eval_jaxpr/ppermute | solution.py:8
  100.5 6.3 %collective-permute-start = (bf16[4,16,256]{2,1,0:T(8,128)(2,1)S(1)}, bf16[4,16,256]{2,1,0:T(8,128)(2,1)S(1)}, u32[]{:S(2)}, u32[]{:S(2)}) collective-permute-start(bf16[4,16,256]{2,1,0:T(8,128)(2,1)S(1)} %fusion.158), channel_id=1, source_target_pairs={{1,0},{2,1},{3,2},{5,4},{6,5},{7,6},{9,8},{10,9},{11,10},{13,12},{... | collective-permute-start | bytes 98312 | tf_op jit(solution)/shard_map/while/body/eval_jaxpr/ppermute | solution.py:19
  101.8 6.4 %collective-permute-start.1 = (bf16[4,16,256]{2,1,0:T(8,128)(2,1)S(1)}, bf16[4,16,256]{2,1,0:T(8,128)(2,1)S(1)}, u32[]{:S(2)}, u32[]{:S(2)}) collective-permute-start(bf16[4,16,256]{2,1,0:T(8,128)(2,1)S(1)} %fusion.158), channel_id=1, source_target_pairs={{0,1},{1,2},{2,3},{4,5},{5,6},{6,7},{8,9},{9,10},{10,11},{12,13},{... | collective-permute-start | bytes 98312 | tf_op jit(solution)/shard_map/while/body/eval_jaxpr/ppermute | solution.py:16
  117.3 10.5 %collective-permute-start.2 = (bf16[4,16,256]{2,1,0:T(8,128)(2,1)S(1)}, bf16[4,16,256]{2,1,0:T(8,128)(2,1)S(1)}, u32[]{:S(2)}, u32[]{:S(2)}) collective-permute-start(bf16[4,16,256]{2,1,0:T(8,128)(2,1)S(1)} %get-tuple-element.463), channel_id=1, source_target_pairs={{0,4},{4,8},{8,12},{12,16},{16,20},{20,24},{24,28},{1,5},{5,9},{9,... | collective-permute-start | bytes 98312 | tf_op jit(solution)/shard_map/while/body/eval_jaxpr/ppermute | solution.py:27
  129.1 6.3 %collective-permute-start = (bf16[4,16,256]{2,1,0:T(8,128)(2,1)S(1)}, bf16[4,16,256]{2,1,0:T(8,128)(2,1)S(1)}, u32[]{:S(2)}, u32[]{:S(2)}) collective-permute-start(bf16[4,16,256]{2,1,0:T(8,128)(2,1)S(1)} %fusion.158), channel_id=1, source_target_pairs={{1,0},{2,1},{3,2},{5,4},{6,5},{7,6},{9,8},{10,9},{11,10},{13,12},{... | collective-permute-start | bytes 98312 | tf_op jit(solution)/shard_map/while/body/eval_jaxpr/ppermute | solution.py:19
  130.4 6.4 %collective-permute-start.1 = (bf16[4,16,256]{2,1,0:T(8,128)(2,1)S(1)}, bf16[4,16,256]{2,1,0:T(8,128)(2,1)S(1)}, u32[]{:S(2)}, u32[]{:S(2)}) collective-permute-start(bf16[4,16,256]{2,1,0:T(8,128)(2,1)S(1)} %fusion.158), channel_id=1, source_target_pairs={{0,1},{1,2},{2,3},{4,5},{5,6},{6,7},{8,9},{9,10},{10,11},{12,13},{... | collective-permute-start | bytes 98312 | tf_op jit(solution)/shard_map/while/body/eval_jaxpr/ppermute | solution.py:16
  145.8 10.5 %collective-permute-start.2 = (bf16[4,16,256]{2,1,0:T(8,128)(2,1)S(1)}, bf16[4,16,256]{2,1,0:T(8,128)(2,1)S(1)}, u32[]{:S(2)}, u32[]{:S(2)}) collective-permute-start(bf16[4,16,256]{2,1,0:T(8,128)(2,1)S(1)} %get-tuple-element.463), channel_id=1, source_target_pairs={{0,4},{4,8},{8,12},{12,16},{16,20},{20,24},{24,28},{1,5},{5,9},{9,... | collective-permute-start | bytes 98312 | tf_op jit(solution)/shard_map/while/body/eval_jaxpr/ppermute | solution.py:27
  157.6 6.3 %collective-permute-start = (bf16[4,16,256]{2,1,0:T(8,128)(2,1)S(1)}, bf16[4,16,256]{2,1,0:T(8,128)(2,1)S(1)}, u32[]{:S(2)}, u32[]{:S(2)}) collective-permute-start(bf16[4,16,256]{2,1,0:T(8,128)(2,1)S(1)} %fusion.158), channel_id=1, source_target_pairs={{1,0},{2,1},{3,2},{5,4},{6,5},{7,6},{9,8},{10,9},{11,10},{13,12},{... | collective-permute-start | bytes 98312 | tf_op jit(solution)/shard_map/while/body/eval_jaxpr/ppermute | solution.py:19
  158.9 6.4 %collective-permute-start.1 = (bf16[4,16,256]{2,1,0:T(8,128)(2,1)S(1)}, bf16[4,16,256]{2,1,0:T(8,128)(2,1)S(1)}, u32[]{:S(2)}, u32[]{:S(2)}) collective-permute-start(bf16[4,16,256]{2,1,0:T(8,128)(2,1)S(1)} %fusion.158), channel_id=1, source_target_pairs={{0,1},{1,2},{2,3},{4,5},{5,6},{6,7},{8,9},{9,10},{10,11},{12,13},{... | collective-permute-start | bytes 98312 | tf_op jit(solution)/shard_map/while/body/eval_jaxpr/ppermute | solution.py:16
  174.4 10.7 %collective-permute-start.2 = (bf16[4,16,256]{2,1,0:T(8,128)(2,1)S(1)}, bf16[4,16,256]{2,1,0:T(8,128)(2,1)S(1)}, u32[]{:S(2)}, u32[]{:S(2)}) collective-permute-start(bf16[4,16,256]{2,1,0:T(8,128)(2,1)S(1)} %get-tuple-element.463), channel_id=1, source_target_pairs={{0,4},{4,8},{8,12},{12,16},{16,20},{20,24},{24,28},{1,5},{5,9},{9,... | collective-permute-start | bytes 98312 | tf_op jit(solution)/shard_map/while/body/eval_jaxpr/ppermute | solution.py:27
  186.3 6.3 %collective-permute-start = (bf16[4,16,256]{2,1,0:T(8,128)(2,1)S(1)}, bf16[4,16,256]{2,1,0:T(8,128)(2,1)S(1)}, u32[]{:S(2)}, u32[]{:S(2)}) collective-permute-start(bf16[4,16,256]{2,1,0:T(8,128)(2,1)S(1)} %fusion.158), channel_id=1, source_target_pairs={{1,0},{2,1},{3,2},{5,4},{6,5},{7,6},{9,8},{10,9},{11,10},{13,12},{... | collective-permute-start | bytes 98312 | tf_op jit(solution)/shard_map/while/body/eval_jaxpr/ppermute | solution.py:19
  187.6 6.4 %collective-permute-start.1 = (bf16[4,16,256]{2,1,0:T(8,128)(2,1)S(1)}, bf16[4,16,256]{2,1,0:T(8,128)(2,1)S(1)}, u32[]{:S(2)}, u32[]{:S(2)}) collective-permute-start(bf16[4,16,256]{2,1,0:T(8,128)(2,1)S(1)} %fusion.158), channel_id=1, source_target_pairs={{0,1},{1,2},{2,3},{4,5},{5,6},{6,7},{8,9},{9,10},{10,11},{12,13},{... | collective-permute-start | bytes 98312 | tf_op jit(solution)/shard_map/while/body/eval_jaxpr/ppermute | solution.py:16
  203.1 10.3 %collective-permute-start.2 = (bf16[4,16,256]{2,1,0:T(8,128)(2,1)S(1)}, bf16[4,16,256]{2,1,0:T(8,128)(2,1)S(1)}, u32[]{:S(2)}, u32[]{:S(2)}) collective-permute-start(bf16[4,16,256]{2,1,0:T(8,128)(2,1)S(1)} %get-tuple-element.463), channel_id=1, source_target_pairs={{0,4},{4,8},{8,12},{12,16},{16,20},{20,24},{24,28},{1,5},{5,9},{9,... | collective-permute-start | bytes 98312 | tf_op jit(solution)/shard_map/while/body/eval_jaxpr/ppermute | solution.py:27
  214.7 6.3 %collective-permute-start = (bf16[4,16,256]{2,1,0:T(8,128)(2,1)S(1)}, bf16[4,16,256]{2,1,0:T(8,128)(2,1)S(1)}, u32[]{:S(2)}, u32[]{:S(2)}) collective-permute-start(bf16[4,16,256]{2,1,0:T(8,128)(2,1)S(1)} %fusion.158), channel_id=1, source_target_pairs={{1,0},{2,1},{3,2},{5,4},{6,5},{7,6},{9,8},{10,9},{11,10},{13,12},{... | collective-permute-start | bytes 98312 | tf_op jit(solution)/shard_map/while/body/eval_jaxpr/ppermute | solution.py:19
  216.0 6.4 %collective-permute-start.1 = (bf16[4,16,256]{2,1,0:T(8,128)(2,1)S(1)}, bf16[4,16,256]{2,1,0:T(8,128)(2,1)S(1)}, u32[]{:S(2)}, u32[]{:S(2)}) collective-permute-start(bf16[4,16,256]{2,1,0:T(8,128)(2,1)S(1)} %fusion.158), channel_id=1, source_target_pairs={{0,1},{1,2},{2,3},{4,5},{5,6},{6,7},{8,9},{9,10},{10,11},{12,13},{... | collective-permute-start | bytes 98312 | tf_op jit(solution)/shard_map/while/body/eval_jaxpr/ppermute | solution.py:16
  231.5 10.3 %collective-permute-start.2 = (bf16[4,16,256]{2,1,0:T(8,128)(2,1)S(1)}, bf16[4,16,256]{2,1,0:T(8,128)(2,1)S(1)}, u32[]{:S(2)}, u32[]{:S(2)}) collective-permute-start(bf16[4,16,256]{2,1,0:T(8,128)(2,1)S(1)} %get-tuple-element.463), channel_id=1, source_target_pairs={{0,4},{4,8},{8,12},{12,16},{16,20},{20,24},{24,28},{1,5},{5,9},{9,... | collective-permute-start | bytes 98312 | tf_op jit(solution)/shard_map/while/body/eval_jaxpr/ppermute | solution.py:27
  243.1 6.3 %collective-permute-start = (bf16[4,16,256]{2,1,0:T(8,128)(2,1)S(1)}, bf16[4,16,256]{2,1,0:T(8,128)(2,1)S(1)}, u32[]{:S(2)}, u32[]{:S(2)}) collective-permute-start(bf16[4,16,256]{2,1,0:T(8,128)(2,1)S(1)} %fusion.158), channel_id=1, source_target_pairs={{1,0},{2,1},{3,2},{5,4},{6,5},{7,6},{9,8},{10,9},{11,10},{13,12},{... | collective-permute-start | bytes 98312 | tf_op jit(solution)/shard_map/while/body/eval_jaxpr/ppermute | solution.py:19
  244.4 6.4 %collective-permute-start.1 = (bf16[4,16,256]{2,1,0:T(8,128)(2,1)S(1)}, bf16[4,16,256]{2,1,0:T(8,128)(2,1)S(1)}, u32[]{:S(2)}, u32[]{:S(2)}) collective-permute-start(bf16[4,16,256]{2,1,0:T(8,128)(2,1)S(1)} %fusion.158), channel_id=1, source_target_pairs={{0,1},{1,2},{2,3},{4,5},{5,6},{6,7},{8,9},{9,10},{10,11},{12,13},{... | collective-permute-start | bytes 98312 | tf_op jit(solution)/shard_map/while/body/eval_jaxpr/ppermute | solution.py:16
  259.9 10.3 %collective-permute-start.2 = (bf16[4,16,256]{2,1,0:T(8,128)(2,1)S(1)}, bf16[4,16,256]{2,1,0:T(8,128)(2,1)S(1)}, u32[]{:S(2)}, u32[]{:S(2)}) collective-permute-start(bf16[4,16,256]{2,1,0:T(8,128)(2,1)S(1)} %get-tuple-element.463), channel_id=1, source_target_pairs={{0,4},{4,8},{8,12},{12,16},{16,20},{20,24},{24,28},{1,5},{5,9},{9,... | collective-permute-start | bytes 98312 | tf_op jit(solution)/shard_map/while/body/eval_jaxpr/ppermute | solution.py:27
  (34 other events, 190.2 us)
where the time goes:
time: 281 us; the launch traced here: 278 us
  starting transfers between devices  102 us (36%)
  waiting for transfers between devices  73.1 us (26%)
  matrix products  70.5 us (25%)
  other arithmetic  10.7 us (4%)
  local copies, waits for them, and re-layouts  10.1 us (4%)
  blocking collectives  7.4 us (3%)
  loops' own time  4.31 us (2%)
    ppermute x30, waiting for transfers between devices, partner(): lax.ppermute(shard, axis, [(i, i ^ 1 << stride) for i in range(lax.axis_s...  60.2 us
    conv_general_dilated x36, matrix products, conv_rows(): lax.conv_general_dilated(extended[None], kernel, (1, 1), ((0, 0), (1, 1))...  59.5 us
    ppermute x9, starting transfers between devices, padded(): lax.ppermute(lax.slice_in_dim(block, block.shape[dim] - width, None, axis...  43.3 us
    ppermute x30, starting transfers between devices, partner(): lax.ppermute(shard, axis, [(i, i ^ 1 << stride) for i in range(lax.axis_s...  25.7 us
    ppermute x9, starting transfers between devices, shifted(): lax.ppermute(value, axis, [(source, source + steps) for source in range(l...  21.5 us
    ppermute x9, waiting for transfers between devices, padded(): lax.ppermute(lax.slice_in_dim(block, block.shape[dim] - width, None, axis...  12.9 us
    ppermute x9, starting transfers between devices, padded(): lax.ppermute(lax.slice_in_dim(block, 0, width, axis=dim), axis, backward)  11.6 us
    dot_general x9, matrix products, run_tick(): jnp.dot(source, own_join, preferred_element_type=jnp.float32)  9.66 us
  transfers between devices with their start and end apart: 57, of which 30 were waited for; matrix products, arithmetic and copies ran while one was open for 1% of the time, Pallas kernels for 0%

commit v1 on v0

v1 whole, which is shorter than its diff:
```python
import functools

import jax
import jax.numpy as jnp
from jax import lax
from jax.experimental import pallas as pl
from jax.experimental.pallas import tpu as pltpu
from jax.sharding import PartitionSpec as P

MESH = pl.DeviceIdType.MESH
HALVES = 2


def unit(values):
    return values * lax.rsqrt(jnp.mean(values * values, axis=-1, keepdims=True) + 1e-05)


def kernel(
    segments,
    bands,
    pix_ref,
    conv_ref,
    join_ref,
    out_ref,
    pix_buf,
    in_buf,
    skip_buf,
    weight_buf,
    own_join,
    mirror_join,
    skip_part,
    own_out,
    halo_out,
    place,
    fin_src,
    fin_dst,
    weight_sem,
    join_sem,
    pix_send,
    pix_recv,
    in_send,
    in_recv,
    skip_send,
    skip_recv,
    mirror_send,
    mirror_recv,
    fin_send,
    fin_recv,
):
    batches, band_rows, columns, channels = pix_ref.shape
    layers = conv_ref.shape[0]
    workers = HALVES * batches
    chunks = pix_buf.shape[0]
    own_px = own_out.shape[0]
    halo_px = halo_out.shape[0]
    half_bands = bands // HALVES
    halfway = segments // 2
    last = segments - 1
    share = columns // segments
    seg = lax.axis_index("segment")
    band = lax.axis_index("band")
    lower = lax.rem(band, HALVES)
    micro = lax.div(band, HALVES)
    other = band + 1 - 2 * lower
    works = band < workers
    own_half = lax.div(band, half_bands)

    weight_copies = []
    for layer in range(layers):
        for dy in range(3):
            to = dy + lower * (2 - 2 * dy)
            weight_copies.append(
                pltpu.make_async_copy(
                    conv_ref.at[layer, dy], weight_buf.at[layer, to], weight_sem.at[layer, dy]
                )
            )
    join_copy = pltpu.make_async_copy(join_ref, own_join, join_sem)

    @pl.when(works)
    def _():
        for copy in weight_copies:
            copy.start()
        join_copy.start()

    barrier = pltpu.get_barrier_semaphore()

    def greet(to_seg, to_band):
        pl.semaphore_signal(barrier, inc=1, device_id=(to_seg, to_band), device_id_type=MESH)

    def chunk_band(chunk):
        return chunk + lower * (bands - 1 - 2 * chunk)

    @pl.when(works & (seg == 0))
    def _():
        for chunk in range(chunks):

            @pl.when(chunk_band(chunk) != band)
            def _():
                greet(0, chunk_band(chunk))

    @pl.when(works & (seg > 0))
    def _():
        greet(seg - 1, band)
        greet(seg - 1, other)

    @pl.when(works & (seg > halfway))
    def _():
        greet(last - seg, band)
        greet(last - seg, other)

    for m in range(batches):

        @pl.when((seg != last) | (band != HALVES * m + own_half))
        def _():
            greet(last, HALVES * m + own_half)

    def one_if(condition):
        return jnp.where(condition, 1, 0).astype(jnp.int32)

    def pix_chunk(worker):
        return band if worker % HALVES == 0 else bands - 1 - band

    def pix_sends(worker):
        return (seg == 0) & (pix_chunk(worker) < chunks) & (band != worker)

    expected = one_if(works & (seg < last)) * 2 + one_if(works & (seg < halfway - 1)) * 2
    for worker in range(workers):
        expected += one_if(pix_sends(worker))
    expected += one_if(works & (seg == last)) * (
        segments * half_bands - one_if(own_half == lower)
    )

    @pl.when(expected > 0)
    def _():
        pl.semaphore_wait(barrier, expected)

    def pix_copy(worker):
        return pltpu.make_async_remote_copy(
            src_ref=pix_ref.at[worker // HALVES],
            dst_ref=pix_buf.at[pix_chunk(worker)],
            send_sem=pix_send.at[worker],
            recv_sem=pix_recv.at[pix_chunk(worker)],
            device_id=(0, worker),
            device_id_type=MESH,
        )

    own_chunk = band + lower * (bands - 1 - 2 * band)
    for worker in range(workers):

        @pl.when(pix_sends(worker))
        def _():
            pix_copy(worker).start()

    @pl.when(works & (seg == 0) & (own_chunk < chunks))
    def _():
        pltpu.make_async_copy(
            pix_ref.at[micro], pix_buf.at[own_chunk], pix_recv.at[own_chunk]
        ).start()

    mirror_copy = pltpu.make_async_remote_copy(
        src_ref=join_ref,
        dst_ref=mirror_join,
        send_sem=mirror_send,
        recv_sem=mirror_recv,
        device_id=(last - seg, band),
        device_id_type=MESH,
    )

    @pl.when(works & (seg < halfway))
    def _():
        mirror_copy.start()

    def hop_copies(buffer, to_seg, send, recv):
        return (
            pltpu.make_async_remote_copy(
                src_ref=own_out,
                dst_ref=buffer.at[pl.ds(0, own_px)],
                send_sem=send.at[0],
                recv_sem=recv.at[0],
                device_id=(to_seg, band),
                device_id_type=MESH,
            ),
            pltpu.make_async_remote_copy(
                src_ref=halo_out,
                dst_ref=buffer.at[pl.ds(own_px, halo_px)],
                send_sem=send.at[1],
                recv_sem=recv.at[1],
                device_id=(to_seg, other),
                device_id_type=MESH,
            ),
        )

    next_copies = hop_copies(in_buf, seg + 1, in_send, in_recv)
    skip_copies = hop_copies(skip_buf, last - seg, skip_send, skip_recv)

    def fin_copy(g, k):
        return pltpu.make_async_remote_copy(
            src_ref=fin_src.at[g * half_bands + k],
            dst_ref=fin_dst.at[micro],
            send_sem=fin_send.at[g * half_bands + k],
            recv_sem=fin_recv.at[micro],
            device_id=(g, chunk_band(k)),
            device_id_type=MESH,
        )

    def dot(a, b):
        return jnp.dot(a, b, preferred_element_type=jnp.float32)

    @pl.when(works)
    def _():
        @pl.when(seg == last)
        def _():
            block_rows = fin_src.shape[1]
            at = lax.broadcasted_iota(jnp.int32, (block_rows, own_px), 0)
            pixel = lax.broadcasted_iota(jnp.int32, (block_rows, own_px), 1)
            row = jnp.zeros_like(at)
            for step in range(1, band_rows):
                row += jnp.where(at >= step * share, 1, 0)
            column = at - row * share
            row = row + lower * (band_rows - 1 - 2 * row)
            inside = at < band_rows * share
            base = row * columns + column
            for g in range(segments):
                for k in range(half_bands):
                    wanted = base + (k * band_rows * columns + g * share)
                    place[g * half_bands + k] = jnp.where(
                        inside & (pixel == wanted), 1.0, 0.0
                    ).astype(jnp.bfloat16)

        join_copy.wait()

        @pl.when(seg >= halfway)
        def _():
            mirror_copy.wait_recv()

        @pl.when(seg > halfway)
        def _():
            for copy in skip_copies:
                copy.wait_recv()
            skip_part[...] = dot(skip_buf[...], mirror_join[...])

        @pl.when(seg == 0)
        def _():
            for chunk in range(chunks):
                pltpu.make_async_copy(
                    pix_ref.at[0], pix_buf.at[chunk], pix_recv.at[chunk]
                ).wait()
            for row in range((own_px + halo_px) // columns):
                within = row % band_rows
                within = within + lower * (band_rows - 1 - 2 * within)
                in_buf[pl.ds(row * columns, columns)] = pix_buf[row // band_rows, within]

        @pl.when(seg > 0)
        def _():
            for copy in next_copies:
                copy.wait_recv()

        @pl.when(seg == halfway)
        def _():
            skip_part[...] = dot(in_buf[...], mirror_join[...])

        @pl.when(seg >= halfway)
        def _():
            in_buf[...] = (skip_part[...] + dot(in_buf[...], own_join[...])).astype(jnp.bfloat16)

        hidden = in_buf[...]
        for layer in range(layers):
            values = hidden.astype(jnp.float32)
            count = values.shape[0]
            scaled = unit(values)
            at = lax.rem(lax.broadcasted_iota(jnp.int32, (count, channels), 0), columns)
            left = jnp.where(at == 0, 0.0, pltpu.roll(scaled, 1, 0))
            right = jnp.where(at == columns - 1, 0.0, pltpu.roll(scaled, count - 1, 0))
            wide = jnp.concatenate(
                [part.astype(jnp.bfloat16) for part in (left, scaled, right)], axis=1
            )
            wide = jnp.concatenate([jnp.zeros((columns, wide.shape[1]), jnp.bfloat16), wide], axis=0)
            keep = count - columns
            for dy in range(3):
                weight_copies[layer * 3 + dy].wait()
            patches = jnp.concatenate(
                [wide[dy * columns : dy * columns + keep] for dy in range(3)], axis=1
            )
            total = dot(patches, weight_buf[layer].reshape(patches.shape[1], channels))
            hidden = (values[:keep] + jnp.maximum(total, 0.0)).astype(jnp.bfloat16)

        @pl.when(seg < last)
        def _():
            own_out[...] = hidden
            for row in range(halo_px // columns):
                start = own_px - (row + 1) * columns
                halo_out[pl.ds(row * columns, columns)] = hidden[start : start + columns]
            for copy in next_copies:
                copy.start()

            @pl.when(seg < halfway - 1)
            def _():
                for copy in skip_copies:
                    copy.start()

        @pl.when(seg == last)
        def _():
            decoded = unit(hidden.astype(jnp.float32)).astype(jnp.bfloat16)
            sorting = place[...].reshape(-1, own_px)
            fin_src[...] = dot(sorting, decoded).astype(jnp.bfloat16).reshape(fin_src.shape)
            for g in range(segments):
                for k in range(half_bands):
                    if g < last:
                        fin_copy(g, k).start()
                    else:
                        here = chunk_band(k) == band

                        @pl.when(here)
                        def _():
                            pltpu.make_async_copy(
                                fin_src.at[g * half_bands + k],
                                fin_dst.at[micro],
                                fin_recv.at[micro],
                            ).start()

                        @pl.when(jnp.logical_not(here))
                        def _():
                            fin_copy(g, k).start()

    for m in range(batches):
        pltpu.make_async_copy(fin_src.at[0], fin_dst.at[m], fin_recv.at[m]).wait()
    out_ref[...] = fin_dst[...]

    for worker in range(workers):

        @pl.when(pix_sends(worker))
        def _():
            pix_copy(worker).wait_send()

    @pl.when(works & (seg < halfway))
    def _():
        mirror_copy.wait_send()

    @pl.when(works & (seg < last))
    def _():
        for copy in next_copies:
            copy.wait_send()

    @pl.when(works & (seg < halfway - 1))
    def _():
        for copy in skip_copies:
            copy.wait_send()

    @pl.when(works & (seg == last))
    def _():
        for g in range(segments):
            for k in range(half_bands):
                if g < last:
                    fin_copy(g, k).wait_send()
                else:

                    @pl.when(chunk_band(k) != band)
                    def _():
                        fin_copy(g, k).wait_send()


def shards(segments, bands, pixels, conv_weight, join_weight):
    batches, band_rows, columns, channels = pixels.shape
    layers = conv_weight.shape[1]
    own_rows = band_rows * bands // HALVES
    rows = own_rows + layers
    chunks = -(-rows // band_rows)
    own_px, halo_px, all_px = own_rows * columns, layers * columns, rows * columns
    share = columns // segments
    piece = band_rows * share
    block_rows = -(-piece // 16) * 16
    blocks = segments * (bands // HALVES)
    workers = HALVES * batches
    kept = jnp.bfloat16
    conv = conv_weight.reshape(layers, 3, 3 * channels, channels)
    join = join_weight.reshape(channels, channels)
    dma = pltpu.SemaphoreType.DMA
    result = pl.pallas_call(
        functools.partial(kernel, segments, bands),
        out_shape=jax.ShapeDtypeStruct((batches, block_rows, channels), kept),
        in_specs=[pl.BlockSpec(memory_space=pl.ANY)] * 3,
        out_specs=pl.BlockSpec(memory_space=pltpu.VMEM),
        scratch_shapes=[
            pltpu.VMEM((chunks, band_rows, columns, channels), kept),
            pltpu.VMEM((all_px, channels), kept),
            pltpu.VMEM((all_px, channels), kept),
            pltpu.VMEM((layers, 3, 3 * channels, channels), kept),
            pltpu.VMEM((channels, channels), kept),
            pltpu.VMEM((channels, channels), kept),
            pltpu.VMEM((all_px, channels), jnp.float32),
            pltpu.VMEM((own_px, channels), kept),
            pltpu.VMEM((halo_px, channels), kept),
            pltpu.VMEM((blocks, block_rows, own_px), kept),
            pltpu.VMEM((blocks, block_rows, channels), kept),
            pltpu.VMEM((batches, block_rows, channels), kept),
            dma((layers, 3)),
            dma,
            dma((workers,)),
            dma((chunks,)),
            dma((2,)),
            dma((2,)),
            dma((2,)),
            dma((2,)),
            dma,
            dma,
            dma((blocks,)),
            dma((batches,)),
        ],
        compiler_params=pltpu.CompilerParams(
            collective_id=0, has_side_effects=True, vmem_limit_bytes=40 * 1024 * 1024
        ),
    )(pixels, conv, join)
    return result[:, :piece].reshape(batches, band_rows, share, channels)


def solution(mesh):
    return jax.shard_map(
        functools.partial(shards, mesh.shape["segment"], mesh.shape["band"]),
        mesh=mesh,
        in_specs=(
            P(None, "band", None, None),
            P("segment", None, None, None, None, None),
            P("segment", None, None),
        ),
        out_specs=P(None, "band", "segment", None),
        check_vma=False,
    )
```

time: 281 us -> 60.9 us (0.22)
  starting transfers between devices: 102 us -> 0 us
  waiting for transfers between devices: 73.1 us -> 0 us
  matrix products: 70.5 us -> 0 us
  Pallas kernels: 0 us -> 56 us
  other arithmetic: 10.7 us -> 0 us
  blocking collectives: 7.4 us -> 0 us
  local copies, waits for them, and re-layouts: 10.1 us -> 4.69 us
  loops' own time: 4.31 us -> 0 us
    ppermute x57 -> x0, starting transfers between devices: 102 us -> none  [the longest x9 43.3 us: padded(): lax.ppermute(lax.slice_in_dim(block, block.shape[dim] - width, None, axis...]
    ppermute x57 -> x0, waiting for transfers between devices: 73.1 us -> none  [the longest x30 60.2 us: partner(): lax.ppermute(shard, axis, [(i, i ^ 1 << stride) for i in range(lax.axis_s...]
    conv_general_dilated x36 -> x0, matrix products: 59.5 us -> none  [conv_rows(): lax.conv_general_dilated(extended[None], kernel, (1, 1), ((0, 0), (1, 1))...]
    pallas_call x0 -> x1, Pallas kernels: none -> 56 us  [shards(): pl.pallas_call(functools.partial(kernel, segments, bands), out_shape=jax....]
    dot_general x18 -> x0, matrix products: 10.9 us -> none  [the longest x9 9.66 us: run_tick(): jnp.dot(source, own_join, preferred_element_type=jnp.float32)]
    all_to_all x1 -> x0, blocking collectives: 7.4 us -> none  [shards(): lax.all_to_all(carried[2], 'segment', split_axis=2, concat_axis=0, tiled=...]
    reduce_sum x45 -> x0, other arithmetic: 6.21 us -> none  [normed(): scale = lax.rsqrt(jnp.mean(values * values, axis=-1, keepdims=True) + 1e-05)]
    max x72 -> x0, local copies, waits for them, and re-layouts: 4.78 us -> none  [conv_rows(): return jnp.maximum(result, 0.0)]
  transfers between devices with their start and end apart: 57 -> 0, of which waited for: 30 -> 0; matrix products, arithmetic and copies ran while one was open for 1% -> 0% of each run, Pallas kernels for 0% -> 0%
where the time goes in v1:
time: 60.9 us; the launch traced here: 60.7 us
  Pallas kernels  56 us (92%)
  local copies, waits for them, and re-layouts  4.69 us (8%)
    pallas_call x1, Pallas kernels, shards(): pl.pallas_call(functools.partial(kernel, segments, bands), out_shape=jax....  56 us
    unnamed x6, local copies, waits for them, and re-layouts  4.08 us

profile of v1, /device:TPU:0, one launch (start us, length us, event | category | flops | bytes accessed | tf_op | source)
XLA Modules:
  0.0 60.7 jit_solution(14588277695074905135)
XLA Ops:
  0.0 0.0 copy-start
  0.0 2.3 %copy-done = bf16[1,4,3,3,256,256]{5,4,3,2,1,0:T(8,128)(2,1)S(1)} copy-done((bf16[1,4,3,3,256,256]{5,4,3,2,1,0:T(8,128)(2,1)S(1)}, bf16[1,4,3,3,256,256]{5,4,3,2,1,0:T(8,128)(2,1)}, u32[]{:S(2)}) %copy-start) | copy-done | bytes 4718616
  2.3 0.0 copy-start.1
  2.3 0.9 %copy-done.1 = bf16[1,256,256]{2,1,0:T(8,128)(2,1)S(1)} copy-done((bf16[1,256,256]{2,1,0:T(8,128)(2,1)S(1)}, bf16[1,256,256]{2,1,0:T(8,128)(2,1)}, u32[]{:S(2)}) %copy-start.1) | copy-done | bytes 131096
  3.2 0.0 copy-start.2
  3.2 0.8 %copy-done.2 = bf16[2,4,16,256]{3,2,1,0:T(8,128)(2,1)S(1)} copy-done((bf16[2,4,16,256]{3,2,1,0:T(8,128)(2,1)S(1)}, bf16[2,4,16,256]{3,2,1,0:T(8,128)(2,1)}, u32[]{:S(2)}) %copy-start.2) | copy-done | bytes 65560
  4.1 56.0 %shard_map.37 = bf16[2,16,256]{2,1,0:T(8,128)(2,1)S(1)} custom-call(bf16[2,4,16,256]{3,2,1,0:T(8,128)(2,1)S(1)} %copy-done.2, bf16[4,3,768,256]{3,2,1,0:T(8,128)(2,1)S(1)} %bitcast.2, bf16[256,256]{1,0:T(8,128)(2,1)S(1)} %bitcast.3), custom_call_target="tpu_custom_call" | custom-call | tf_op jit(solution)/shard_map/pallas_call | solution.py:378
  60.1 0.6 %reshape.11 = bf16[2,4,2,256]{3,2,1,0:T(2,128)(2,1)} reshape(bf16[2,8,256]{2,1,0:T(8,128)(2,1)S(1)} %slice.3) | data formatting | bytes 16384 | tf_op jit(solution)/shard_map/reshape | solution.py:413
  (1 shorter events, 0.0 us)
Async XLA Ops:
  0.0 2.3 %copy-start = (bf16[1,4,3,3,256,256]{5,4,3,2,1,0:T(8,128)(2,1)S(1)}, bf16[1,4,3,3,256,256]{5,4,3,2,1,0:T(8,128)(2,1)}, u32[]{:S(2)}) copy-start(bf16[1,4,3,3,256,256]{5,4,3,2,1,0:T(8,128)(2,1)} %param.4) | copy-start | bytes 14155780
  2.3 0.9 %copy-start.1 = (bf16[1,256,256]{2,1,0:T(8,128)(2,1)S(1)}, bf16[1,256,256]{2,1,0:T(8,128)(2,1)}, u32[]{:S(2)}) copy-start(bf16[1,256,256]{2,1,0:T(8,128)(2,1)} %param.5) | copy-start | bytes 393220
  3.2 0.8 %copy-start.2 = (bf16[2,4,16,256]{3,2,1,0:T(8,128)(2,1)S(1)}, bf16[2,4,16,256]{3,2,1,0:T(8,128)(2,1)}, u32[]{:S(2)}) copy-start(bf16[2,4,16,256]{3,2,1,0:T(8,128)(2,1)} %pix_ref.1) | copy-start | bytes 196612

commit v2 on v1

--- a/solution.py
+++ b/solution.py
@@ -268,7 +268,9 @@
             values = hidden.astype(jnp.float32)
             count = values.shape[0]
             scaled = unit(values)
-            at = lax.rem(lax.broadcasted_iota(jnp.int32, (count, channels), 0), columns)
+            at = lax.broadcasted_iota(
+                jnp.int32, (count // columns, columns, channels), 1
+            ).reshape(count, channels)
             left = jnp.where(at == 0, 0.0, pltpu.roll(scaled, 1, 0))
             right = jnp.where(at == columns - 1, 0.0, pltpu.roll(scaled, count - 1, 0))
             wide = jnp.concatenate(
@@ -378,7 +380,7 @@
     result = pl.pallas_call(
         functools.partial(kernel, segments, bands),
         out_shape=jax.ShapeDtypeStruct((batches, block_rows, channels), kept),
-        in_specs=[pl.BlockSpec(memory_space=pl.ANY)] * 3,
+        in_specs=[pl.BlockSpec(memory_space=pltpu.HBM)] * 3,
         out_specs=pl.BlockSpec(memory_space=pltpu.VMEM),
         scratch_shapes=[
             pltpu.VMEM((chunks, band_rows, columns, channels), kept),

time: 60.9 us -> 60.8 us (level)
  no operation moved by 1% of the time
where the time goes in v2:
time: 60.8 us; the launch traced here: 60.6 us
  Pallas kernels  55.9 us (92%)
  local copies, waits for them, and re-layouts  4.69 us (8%)
    pallas_call x1, Pallas kernels, shards(): pl.pallas_call(functools.partial(kernel, segments, bands), out_shape=jax....  55.9 us
    unnamed x6, local copies, waits for them, and re-layouts  4.08 us

profile of v2, /device:TPU:0, one launch (start us, length us, event | category | flops | bytes accessed | tf_op | source)
XLA Modules:
  0.0 60.6 jit_solution(5745282389919116453)
XLA Ops:
  0.0 0.0 copy-start
  0.0 2.3 %copy-done = bf16[1,4,3,3,256,256]{5,4,3,2,1,0:T(8,128)(2,1)S(1)} copy-done((bf16[1,4,3,3,256,256]{5,4,3,2,1,0:T(8,128)(2,1)S(1)}, bf16[1,4,3,3,256,256]{5,4,3,2,1,0:T(8,128)(2,1)}, u32[]{:S(2)}) %copy-start) | copy-done | bytes 4718616
  2.3 0.0 copy-start.1
  2.3 0.9 %copy-done.1 = bf16[1,256,256]{2,1,0:T(8,128)(2,1)S(1)} copy-done((bf16[1,256,256]{2,1,0:T(8,128)(2,1)S(1)}, bf16[1,256,256]{2,1,0:T(8,128)(2,1)}, u32[]{:S(2)}) %copy-start.1) | copy-done | bytes 131096
  3.2 0.0 copy-start.2
  3.2 0.8 %copy-done.2 = bf16[2,4,16,256]{3,2,1,0:T(8,128)(2,1)S(1)} copy-done((bf16[2,4,16,256]{3,2,1,0:T(8,128)(2,1)S(1)}, bf16[2,4,16,256]{3,2,1,0:T(8,128)(2,1)}, u32[]{:S(2)}) %copy-start.2) | copy-done | bytes 65560
  4.1 55.9 %shard_map.37 = bf16[2,16,256]{2,1,0:T(8,128)(2,1)S(1)} custom-call(bf16[2,4,16,256]{3,2,1,0:T(8,128)(2,1)S(1)} %copy-done.2, bf16[4,3,768,256]{3,2,1,0:T(8,128)(2,1)S(1)} %bitcast.2, bf16[256,256]{1,0:T(8,128)(2,1)S(1)} %bitcast.3), custom_call_target="tpu_custom_call" | custom-call | tf_op jit(solution)/shard_map/pallas_call | solution.py:380
  60.0 0.6 %reshape.11 = bf16[2,4,2,256]{3,2,1,0:T(2,128)(2,1)} reshape(bf16[2,8,256]{2,1,0:T(8,128)(2,1)S(1)} %slice.3) | data formatting | bytes 16384 | tf_op jit(solution)/shard_map/reshape | solution.py:415
  (1 shorter events, 0.0 us)
Async XLA Ops:
  0.0 2.3 %copy-start = (bf16[1,4,3,3,256,256]{5,4,3,2,1,0:T(8,128)(2,1)S(1)}, bf16[1,4,3,3,256,256]{5,4,3,2,1,0:T(8,128)(2,1)}, u32[]{:S(2)}) copy-start(bf16[1,4,3,3,256,256]{5,4,3,2,1,0:T(8,128)(2,1)} %param.4) | copy-start | bytes 14155780
  2.3 0.9 %copy-start.1 = (bf16[1,256,256]{2,1,0:T(8,128)(2,1)S(1)}, bf16[1,256,256]{2,1,0:T(8,128)(2,1)}, u32[]{:S(2)}) copy-start(bf16[1,256,256]{2,1,0:T(8,128)(2,1)} %param.5) | copy-start | bytes 393220
  3.2 0.8 %copy-start.2 = (bf16[2,4,16,256]{3,2,1,0:T(8,128)(2,1)S(1)}, bf16[2,4,16,256]{3,2,1,0:T(8,128)(2,1)}, u32[]{:S(2)}) copy-start(bf16[2,4,16,256]{3,2,1,0:T(8,128)(2,1)} %pix_ref.1) | copy-start | bytes 196612

commit v3 on v2

--- a/solution.py
+++ b/solution.py
@@ -29,6 +29,8 @@
     own_join,
     mirror_join,
     skip_part,
+    hid,
+    wide,
     own_out,
     halo_out,
     place,
@@ -53,6 +55,7 @@
     chunks = pix_buf.shape[0]
     own_px = own_out.shape[0]
     halo_px = halo_out.shape[0]
+    all_px = own_px + halo_px
     half_bands = bands // HALVES
     halfway = segments // 2
     last = segments - 1
@@ -227,7 +230,11 @@
                         inside & (pixel == wanted), 1.0, 0.0
                     ).astype(jnp.bfloat16)
 
+        hid[...] = jnp.zeros_like(hid)
+        wide[pl.ds(0, columns)] = jnp.zeros((columns, wide.shape[1]), jnp.bfloat16)
         join_copy.wait()
+        for copy in weight_copies:
+            copy.wait()
 
         @pl.when(seg >= halfway)
         def _():
@@ -239,52 +246,63 @@
                 copy.wait_recv()
             skip_part[...] = dot(skip_buf[...], mirror_join[...])
 
-        @pl.when(seg == 0)
-        def _():
-            for chunk in range(chunks):
-                pltpu.make_async_copy(
-                    pix_ref.at[0], pix_buf.at[chunk], pix_recv.at[chunk]
-                ).wait()
-            for row in range((own_px + halo_px) // columns):
-                within = row % band_rows
-                within = within + lower * (band_rows - 1 - 2 * within)
-                in_buf[pl.ds(row * columns, columns)] = pix_buf[row // band_rows, within]
-
-        @pl.when(seg > 0)
-        def _():
-            for copy in next_copies:
-                copy.wait_recv()
-
-        @pl.when(seg == halfway)
-        def _():
-            skip_part[...] = dot(in_buf[...], mirror_join[...])
-
-        @pl.when(seg >= halfway)
-        def _():
-            in_buf[...] = (skip_part[...] + dot(in_buf[...], own_join[...])).astype(jnp.bfloat16)
-
-        hidden = in_buf[...]
-        for layer in range(layers):
-            values = hidden.astype(jnp.float32)
-            count = values.shape[0]
-            scaled = unit(values)
-            at = lax.broadcasted_iota(
-                jnp.int32, (count // columns, columns, channels), 1
-            ).reshape(count, channels)
+        def take_input():
+            @pl.when(seg == 0)
+            def _():
+                for chunk in range(chunks):
+                    pltpu.make_async_copy(
+                        pix_ref.at[0], pix_buf.at[chunk], pix_recv.at[chunk]
+                    ).wait()
+                for row in range(all_px // columns):
+                    within = row % band_rows
+                    within = within + lower * (band_rows - 1 - 2 * within)
+                    hid[pl.ds(row * columns, columns)] = pix_buf[row // band_rows, within]
+
+            @pl.when(seg > 0)
+            def _():
+                for copy in next_copies:
+                    copy.wait_recv()
+
+            @pl.when((seg > 0) & (seg < halfway))
+            def _():
+                hid[...] = in_buf[...]
+
+            @pl.when(seg == halfway)
+            def _():
+                skip_part[...] = dot(in_buf[...], mirror_join[...])
+
+            @pl.when(seg >= halfway)
+            def _():
+                hid[...] = (skip_part[...] + dot(in_buf[...], own_join[...])).astype(jnp.bfloat16)
+
+        keep = all_px - columns
+        at = lax.broadcasted_iota(jnp.int32, (all_px // columns, columns, channels), 1).reshape(
+            all_px, channels
+        )
+
+        def step(index, carry):
+            @pl.when(index == 1)
+            def _():
+                take_input()
+
+            layer = jnp.maximum(index - 1, 0)
+            scaled = unit(hid[...].astype(jnp.float32))
             left = jnp.where(at == 0, 0.0, pltpu.roll(scaled, 1, 0))
-            right = jnp.where(at == columns - 1, 0.0, pltpu.roll(scaled, count - 1, 0))
-            wide = jnp.concatenate(
-                [part.astype(jnp.bfloat16) for part in (left, scaled, right)], axis=1
-            )
-            wide = jnp.concatenate([jnp.zeros((columns, wide.shape[1]), jnp.bfloat16), wide], axis=0)
-            keep = count - columns
-            for dy in range(3):
-                weight_copies[layer * 3 + dy].wait()
-            patches = jnp.concatenate(
-                [wide[dy * columns : dy * columns + keep] for dy in range(3)], axis=1
-            )
-            total = dot(patches, weight_buf[layer].reshape(patches.shape[1], channels))
-            hidden = (values[:keep] + jnp.maximum(total, 0.0)).astype(jnp.bfloat16)
+            right = jnp.where(at == columns - 1, 0.0, pltpu.roll(scaled, all_px - 1, 0))
+            for place_at, part in enumerate((left, scaled, right)):
+                wide[pl.ds(columns, all_px), pl.ds(place_at * channels, channels)] = part.astype(
+                    jnp.bfloat16
+                )
+            total = dot(wide[pl.ds(0, keep)], weight_buf[layer, 0])
+            for dy in range(1, 3):
+                total += dot(wide[pl.ds(dy * columns, keep)], weight_buf[layer, dy])
+            hid[pl.ds(0, keep)] = (
+                hid[pl.ds(0, keep)].astype(jnp.float32) + jnp.maximum(total, 0.0)
+            ).astype(jnp.bfloat16)
+            return carry
+
+        lax.fori_loop(0, layers + 1, step, 0)
+        hidden = hid[pl.ds(0, own_px)]
 
         @pl.when(seg < last)
         def _():
@@ -390,6 +408,8 @@
             pltpu.VMEM((channels, channels), kept),
             pltpu.VMEM((channels, channels), kept),
             pltpu.VMEM((all_px, channels), jnp.float32),
+            pltpu.VMEM((all_px, channels), kept),
+            pltpu.VMEM((all_px + columns, 3 * channels), kept),
             pltpu.VMEM((own_px, channels), kept),
             pltpu.VMEM((halo_px, channels), kept),
             pltpu.VMEM((blocks, block_rows, own_px), kept),
@@ -408,9 +428,7 @@
             dma((blocks,)),
             dma((batches,)),
         ],
-        compiler_params=pltpu.CompilerParams(
-            collective_id=0, has_side_effects=True, vmem_limit_bytes=40 * 1024 * 1024
-        ),
+        compiler_params=pltpu.CompilerParams(collective_id=0, has_side_effects=True),
     )(pixels, conv, join)
     return result[:, :piece].reshape(batches, band_rows, share, channels)
 

time: 60.8 us -> 51.5 us (0.85)
  Pallas kernels: 55.9 us -> 49.9 us
  local copies, waits for them, and re-layouts: 4.69 us -> 1.31 us
    pallas_call x1, Pallas kernels: 55.9 us -> 49.9 us  [shards(): pl.pallas_call(functools.partial(kernel, segments, bands), out_shape=jax....]
    unnamed x6 -> x0, local copies, waits for them, and re-layouts: 4.08 us -> none
    slice x1, local copies, waits for them, and re-layouts: 0.01 us -> 0.7 us  [shards(): return result[:, :piece].reshape(batches, band_rows, share, channels)]
where the time goes in v3:
time: 51.5 us; the launch traced here: 51.2 us
  Pallas kernels  49.9 us (97%)
  local copies, waits for them, and re-layouts  1.31 us (3%)
    pallas_call x1, Pallas kernels, shards(): pl.pallas_call(functools.partial(kernel, segments, bands), out_shape=jax....  49.9 us

profile of v3, /device:TPU:0, one launch (start us, length us, event | category | flops | bytes accessed | tf_op | source)
XLA Modules:
  0.0 51.2 jit_solution(1722201038647823967)
XLA Ops:
  0.0 49.9 %shard_map.37 = bf16[2,16,256]{2,1,0:T(8,128)(2,1)} custom-call(bf16[2,4,16,256]{3,2,1,0:T(8,128)(2,1)} %pix_ref.1, bf16[4,3,768,256]{3,2,1,0:T(8,128)(2,1)} %bitcast.2, bf16[256,256]{1,0:T(8,128)(2,1)} %bitcast.3), custom_call_target="tpu_custom_call" | custom-call | tf_op jit(solution)/shard_map/pallas_call | solution.py:398
  49.9 0.7 %slice.3 = bf16[2,8,256]{2,1,0:T(8,128)(2,1)S(1)} slice(bf16[2,16,256]{2,1,0:T(8,128)(2,1)} %shard_map.37), slice={[0:2], [0:8], [0:256]} | slice | bytes 16384 | tf_op jit(solution)/shard_map/slice | solution.py:433
  50.6 0.6 %reshape.11 = bf16[2,4,2,256]{3,2,1,0:T(2,128)(2,1)} reshape(bf16[2,8,256]{2,1,0:T(8,128)(2,1)S(1)} %slice.3) | data formatting | bytes 16384 | tf_op jit(solution)/shard_map/reshape | solution.py:433

commit v4 on v3

--- a/solution.py
+++ b/solution.py
@@ -30,7 +30,7 @@
     mirror_join,
     skip_part,
     hid,
-    wide,
+    patches,
     own_out,
     halo_out,
     place,
@@ -231,10 +231,14 @@
                     ).astype(jnp.bfloat16)
 
         hid[...] = jnp.zeros_like(hid)
-        wide[pl.ds(0, columns)] = jnp.zeros((columns, wide.shape[1]), jnp.bfloat16)
+        span = 3 * channels
+        patches[pl.ds(0, columns), pl.ds(0, span)] = jnp.zeros((columns, span), jnp.bfloat16)
         join_copy.wait()
-        for copy in weight_copies:
-            copy.wait()
+
+        @pl.when(seg > 0)
+        def _():
+            for copy in weight_copies:
+                copy.wait()
 
         @pl.when(seg >= halfway)
         def _():
@@ -286,31 +290,40 @@
                 take_input()
 
             layer = jnp.maximum(index - 1, 0)
+
+            @pl.when(seg == 0)
+            def _():
+                for dy in range(3):
+                    pltpu.make_async_copy(
+                        conv_ref.at[layer, dy], weight_buf.at[layer, dy], weight_sem.at[layer, dy]
+                    ).wait()
+
             scaled = unit(hid[...].astype(jnp.float32))
             left = jnp.where(at == 0, 0.0, pltpu.roll(scaled, 1, 0))
             right = jnp.where(at == columns - 1, 0.0, pltpu.roll(scaled, all_px - 1, 0))
-            for place_at, part in enumerate((left, scaled, right)):
-                wide[pl.ds(columns, all_px), pl.ds(place_at * channels, channels)] = part.astype(
-                    jnp.bfloat16
-                )
-            total = dot(wide[pl.ds(0, keep)], weight_buf[layer, 0])
-            for dy in range(1, 3):
-                total += dot(wide[pl.ds(dy * columns, keep)], weight_buf[layer, dy])
+            for dx, part in enumerate((left, scaled, right)):
+                part = part.astype(jnp.bfloat16)
+                patches[pl.ds(columns, keep - columns), pl.ds(dx * channels, channels)] = part[
+                    : keep - columns
+                ]
+                patches[:, pl.ds(span + dx * channels, channels)] = part[:keep]
+                patches[:, pl.ds(2 * span + dx * channels, channels)] = part[columns:]
+            total = dot(patches[...], weight_buf[layer].reshape(3 * span, channels))
             hid[pl.ds(0, keep)] = (
                 hid[pl.ds(0, keep)].astype(jnp.float32) + jnp.maximum(total, 0.0)
             ).astype(jnp.bfloat16)
             return carry
 
-        lax.fori_loop(0, layers + 1, step, 0)
+        lax.fori_loop(one_if(seg == 0), layers + 1, step, 0)
         hidden = hid[pl.ds(0, own_px)]
 
         @pl.when(seg < last)
         def _():
-            own_out[...] = hidden
             for row in range(halo_px // columns):
                 start = own_px - (row + 1) * columns
                 halo_out[pl.ds(row * columns, columns)] = hidden[start : start + columns]
-            for copy in next_copies:
+            own_out[...] = hidden
+            for copy in next_copies[::-1]:
                 copy.start()
 
             @pl.when(seg < halfway - 1)
@@ -344,7 +357,7 @@
 
     for m in range(batches):
         pltpu.make_async_copy(fin_src.at[0], fin_dst.at[m], fin_recv.at[m]).wait()
-    out_ref[...] = fin_dst[...]
+    out_ref[...] = fin_dst[:, : out_ref.shape[1]]
 
     for worker in range(workers):
 
@@ -397,7 +410,7 @@
     dma = pltpu.SemaphoreType.DMA
     result = pl.pallas_call(
         functools.partial(kernel, segments, bands),
-        out_shape=jax.ShapeDtypeStruct((batches, block_rows, channels), kept),
+        out_shape=jax.ShapeDtypeStruct((batches, piece, channels), kept),
         in_specs=[pl.BlockSpec(memory_space=pltpu.HBM)] * 3,
         out_specs=pl.BlockSpec(memory_space=pltpu.VMEM),
         scratch_shapes=[
@@ -409,7 +422,7 @@
             pltpu.VMEM((channels, channels), kept),
             pltpu.VMEM((all_px, channels), jnp.float32),
             pltpu.VMEM((all_px, channels), kept),
-            pltpu.VMEM((all_px + columns, 3 * channels), kept),
+            pltpu.VMEM((all_px - columns, 9 * channels), kept),
             pltpu.VMEM((own_px, channels), kept),
             pltpu.VMEM((halo_px, channels), kept),
             pltpu.VMEM((blocks, block_rows, own_px), kept),
@@ -430,7 +443,7 @@
         ],
         compiler_params=pltpu.CompilerParams(collective_id=0, has_side_effects=True),
     )(pixels, conv, join)
-    return result[:, :piece].reshape(batches, band_rows, share, channels)
+    return result.reshape(batches, band_rows, share, channels)
 
 
 def solution(mesh):

time: 51.5 us -> 51.4 us (level)
    slice x1 -> x0, local copies, waits for them, and re-layouts: 0.7 us -> none  [shards(): return result[:, :piece].reshape(batches, band_rows, share, channels)]
    reshape x1, local copies, waits for them, and re-layouts: 0.61 us -> 1.31 us  [shards(): return result.reshape(batches, band_rows, share, channels)]
where the time goes in v4:
time: 51.4 us; the launch traced here: 51.2 us
  Pallas kernels  49.9 us (97%)
  local copies, waits for them, and re-layouts  1.31 us (3%)
    pallas_call x1, Pallas kernels, shards(): pl.pallas_call(functools.partial(kernel, segments, bands), out_shape=jax....  49.9 us
    reshape x1, local copies, waits for them, and re-layouts, shards(): return result.reshape(batches, band_rows, share, channels)  1.31 us

profile of v4, /device:TPU:0, one launch (start us, length us, event | category | flops | bytes accessed | tf_op | source)
XLA Modules:
  0.0 51.2 jit_solution(6621768597010249935)
XLA Ops:
  0.0 49.9 %shard_map.37 = bf16[2,8,256]{2,1,0:T(8,128)(2,1)} custom-call(bf16[2,4,16,256]{3,2,1,0:T(8,128)(2,1)} %pix_ref.1, bf16[4,3,768,256]{3,2,1,0:T(8,128)(2,1)} %bitcast.2, bf16[256,256]{1,0:T(8,128)(2,1)} %bitcast.3), custom_call_target="tpu_custom_call" | custom-call | tf_op jit(solution)/shard_map/pallas_call | solution.py:411
  49.9 1.3 %reshape.11 = bf16[2,4,2,256]{3,2,1,0:T(2,128)(2,1)} reshape(bf16[2,8,256]{2,1,0:T(8,128)(2,1)} %shard_map.37) | data formatting | bytes 16384 | tf_op jit(solution)/shard_map/reshape | solution.py:446

commit v5 on v4

--- a/solution.py
+++ b/solution.py
@@ -30,7 +30,7 @@
     mirror_join,
     skip_part,
     hid,
-    patches,
+    wide,
     own_out,
     halo_out,
     place,
@@ -232,7 +232,7 @@
 
         hid[...] = jnp.zeros_like(hid)
         span = 3 * channels
-        patches[pl.ds(0, columns), pl.ds(0, span)] = jnp.zeros((columns, span), jnp.bfloat16)
+        wide[pl.ds(0, columns)] = jnp.zeros((columns, span), jnp.bfloat16)
         join_copy.wait()
 
         @pl.when(seg > 0)
@@ -284,6 +284,9 @@
             all_px, channels
         )
 
+        first = -(-keep // (2 * columns)) * columns
+        blocks = ((0, first), (first, keep - first))
+
         def step(index, carry):
             @pl.when(index == 1)
             def _():
@@ -302,16 +305,16 @@
             left = jnp.where(at == 0, 0.0, pltpu.roll(scaled, 1, 0))
             right = jnp.where(at == columns - 1, 0.0, pltpu.roll(scaled, all_px - 1, 0))
             for dx, part in enumerate((left, scaled, right)):
-                part = part.astype(jnp.bfloat16)
-                patches[pl.ds(columns, keep - columns), pl.ds(dx * channels, channels)] = part[
-                    : keep - columns
-                ]
-                patches[:, pl.ds(span + dx * channels, channels)] = part[:keep]
-                patches[:, pl.ds(2 * span + dx * channels, channels)] = part[columns:]
-            total = dot(patches[...], weight_buf[layer].reshape(3 * span, channels))
-            hid[pl.ds(0, keep)] = (
-                hid[pl.ds(0, keep)].astype(jnp.float32) + jnp.maximum(total, 0.0)
-            ).astype(jnp.bfloat16)
+                wide[pl.ds(columns, all_px), pl.ds(dx * channels, channels)] = part.astype(
+                    jnp.bfloat16
+                )
+            for start, size in blocks:
+                total = dot(wide[pl.ds(start, size)], weight_buf[layer, 0])
+                for dy in range(1, 3):
+                    total += dot(wide[pl.ds(start + dy * columns, size)], weight_buf[layer, dy])
+                hid[pl.ds(start, size)] = (
+                    hid[pl.ds(start, size)].astype(jnp.float32) + jnp.maximum(total, 0.0)
+                ).astype(jnp.bfloat16)
             return carry
 
         lax.fori_loop(one_if(seg == 0), layers + 1, step, 0)
@@ -422,7 +425,7 @@
             pltpu.VMEM((channels, channels), kept),
             pltpu.VMEM((all_px, channels), jnp.float32),
             pltpu.VMEM((all_px, channels), kept),
-            pltpu.VMEM((all_px - columns, 9 * channels), kept),
+            pltpu.VMEM((all_px + columns, 3 * channels), kept),
             pltpu.VMEM((own_px, channels), kept),
             pltpu.VMEM((halo_px, channels), kept),
             pltpu.VMEM((blocks, block_rows, own_px), kept),

time: 51.4 us -> 55.8 us (1.086)
  Pallas kernels: 49.9 us -> 54.2 us
    pallas_call x1, Pallas kernels: 49.9 us -> 54.2 us  [shards(): pl.pallas_call(functools.partial(kernel, segments, bands), out_shape=jax....]
where the time goes in v5:
time: 55.8 us; the launch traced here: 55.5 us
  Pallas kernels  54.2 us (97%)
  local copies, waits for them, and re-layouts  1.31 us (2%)
    pallas_call x1, Pallas kernels, shards(): pl.pallas_call(functools.partial(kernel, segments, bands), out_shape=jax....  54.2 us
    reshape x1, local copies, waits for them, and re-layouts, shards(): return result.reshape(batches, band_rows, share, channels)  1.31 us

profile of v5, /device:TPU:0, one launch (start us, length us, event | category | flops | bytes accessed | tf_op | source)
XLA Modules:
  0.0 55.5 jit_solution(5411725492393941512)
XLA Ops:
  0.0 54.2 %shard_map.37 = bf16[2,8,256]{2,1,0:T(8,128)(2,1)} custom-call(bf16[2,4,16,256]{3,2,1,0:T(8,128)(2,1)} %pix_ref.1, bf16[4,3,768,256]{3,2,1,0:T(8,128)(2,1)} %bitcast.2, bf16[256,256]{1,0:T(8,128)(2,1)} %bitcast.3), custom_call_target="tpu_custom_call" | custom-call | tf_op jit(solution)/shard_map/pallas_call | solution.py:414
  54.2 1.3 %reshape.11 = bf16[2,4,2,256]{3,2,1,0:T(2,128)(2,1)} reshape(bf16[2,8,256]{2,1,0:T(8,128)(2,1)} %shard_map.37) | data formatting | bytes 16384 | tf_op jit(solution)/shard_map/reshape | solution.py:449

commit v6 on v4

--- a/solution.py
+++ b/solution.py
@@ -30,7 +30,7 @@
     mirror_join,
     skip_part,
     hid,
-    patches,
+    wide,
     own_out,
     halo_out,
     place,
@@ -231,8 +231,7 @@
                     ).astype(jnp.bfloat16)
 
         hid[...] = jnp.zeros_like(hid)
-        span = 3 * channels
-        patches[pl.ds(0, columns), pl.ds(0, span)] = jnp.zeros((columns, span), jnp.bfloat16)
+        wide[:, pl.ds(0, columns)] = jnp.zeros((3, columns, channels), jnp.bfloat16)
         join_copy.wait()
 
         @pl.when(seg > 0)
@@ -284,6 +283,7 @@
             all_px, channels
         )
 
+
         def step(index, carry):
             @pl.when(index == 1)
             def _():
@@ -299,16 +299,19 @@
                     ).wait()
 
             scaled = unit(hid[...].astype(jnp.float32))
-            left = jnp.where(at == 0, 0.0, pltpu.roll(scaled, 1, 0))
-            right = jnp.where(at == columns - 1, 0.0, pltpu.roll(scaled, all_px - 1, 0))
-            for dx, part in enumerate((left, scaled, right)):
-                part = part.astype(jnp.bfloat16)
-                patches[pl.ds(columns, keep - columns), pl.ds(dx * channels, channels)] = part[
-                    : keep - columns
-                ]
-                patches[:, pl.ds(span + dx * channels, channels)] = part[:keep]
-                patches[:, pl.ds(2 * span + dx * channels, channels)] = part[columns:]
-            total = dot(patches[...], weight_buf[layer].reshape(3 * span, channels))
+            total = jnp.zeros((keep, channels), jnp.float32)
+            for dx in (1, 0, 2):
+                part = scaled
+                if dx == 0:
+                    part = jnp.where(at == 0, 0.0, pltpu.roll(scaled, 1, 0))
+                if dx == 2:
+                    part = jnp.where(at == columns - 1, 0.0, pltpu.roll(scaled, all_px - 1, 0))
+                wide[dx, pl.ds(columns, all_px)] = part.astype(jnp.bfloat16)
+                for dy in range(3):
+                    total += dot(
+                        wide[dx, pl.ds(dy * columns, keep)],
+                        weight_buf[layer, dy, pl.ds(dx * channels, channels)],
+                    )
             hid[pl.ds(0, keep)] = (
                 hid[pl.ds(0, keep)].astype(jnp.float32) + jnp.maximum(total, 0.0)
             ).astype(jnp.bfloat16)
@@ -422,7 +425,7 @@
             pltpu.VMEM((channels, channels), kept),
             pltpu.VMEM((all_px, channels), jnp.float32),
             pltpu.VMEM((all_px, channels), kept),
-            pltpu.VMEM((all_px - columns, 9 * channels), kept),
+            pltpu.VMEM((3, all_px + columns, channels), kept),
             pltpu.VMEM((own_px, channels), kept),
             pltpu.VMEM((halo_px, channels), kept),
             pltpu.VMEM((blocks, block_rows, own_px), kept),

time: 51.4 us -> 51.4 us (level)
  no operation moved by 1% of the time
where the time goes in v6:
time: 51.4 us; the launch traced here: 51.2 us
  Pallas kernels  49.9 us (97%)
  local copies, waits for them, and re-layouts  1.31 us (3%)
    pallas_call x1, Pallas kernels, shards(): pl.pallas_call(functools.partial(kernel, segments, bands), out_shape=jax....  49.9 us
    reshape x1, local copies, waits for them, and re-layouts, shards(): return result.reshape(batches, band_rows, share, channels)  1.31 us

profile of v6, /device:TPU:0, one launch (start us, length us, event | category | flops | bytes accessed | tf_op | source)
XLA Modules:
  0.0 51.2 jit_solution(9700802010710997846)
XLA Ops:
  0.0 49.9 %shard_map.37 = bf16[2,8,256]{2,1,0:T(8,128)(2,1)} custom-call(bf16[2,4,16,256]{3,2,1,0:T(8,128)(2,1)} %pix_ref.1, bf16[4,3,768,256]{3,2,1,0:T(8,128)(2,1)} %bitcast.2, bf16[256,256]{1,0:T(8,128)(2,1)} %bitcast.3), custom_call_target="tpu_custom_call" | custom-call | tf_op jit(solution)/shard_map/pallas_call | solution.py:414
  49.9 1.3 %reshape.11 = bf16[2,4,2,256]{3,2,1,0:T(2,128)(2,1)} reshape(bf16[2,8,256]{2,1,0:T(8,128)(2,1)} %shard_map.37) | data formatting | bytes 16384 | tf_op jit(solution)/shard_map/reshape | solution.py:449

commit v7 on v5

--- a/solution.py
+++ b/solution.py
@@ -25,6 +25,8 @@
     pix_buf,
     in_buf,
     skip_buf,
+    early_skip,
+    early_out,
     weight_buf,
     own_join,
     mirror_join,
@@ -46,6 +48,10 @@
     skip_recv,
     mirror_send,
     mirror_recv,
+    feed_send,
+    feed_recv,
+    early_send,
+    early_recv,
     fin_send,
     fin_recv,
 ):
@@ -59,13 +65,15 @@
     half_bands = bands // HALVES
     halfway = segments // 2
     last = segments - 1
+    tail = segments - 2
     share = columns // segments
     seg = lax.axis_index("segment")
     band = lax.axis_index("band")
     lower = lax.rem(band, HALVES)
     micro = lax.div(band, HALVES)
     other = band + 1 - 2 * lower
-    works = band < workers
+    works = (band < workers) & (lax.rem(seg, 2) == 0)
+    feeds = (band < workers) & (lax.rem(seg, 2) == 1)
     own_half = lax.div(band, half_bands)
 
     weight_copies = []
@@ -77,7 +85,7 @@
                     conv_ref.at[layer, dy], weight_buf.at[layer, to], weight_sem.at[layer, dy]
                 )
             )
-    join_copy = pltpu.make_async_copy(join_ref, own_join, join_sem)
+    join_copy = pltpu.make_async_copy(join_ref, own_join.at[0], join_sem)
 
     @pl.when(works)
     def _():
@@ -101,21 +109,29 @@
             def _():
                 greet(0, chunk_band(chunk))
 
+    @pl.when(works)
+    def _():
+        greet(seg + 1, band)
+
     @pl.when(works & (seg > 0))
     def _():
-        greet(seg - 1, band)
-        greet(seg - 1, other)
+        greet(seg - 2, band)
+        greet(seg - 2, other)
 
     @pl.when(works & (seg > halfway))
     def _():
+        greet(tail - seg, band)
+        greet(tail - seg, other)
+
+    @pl.when(works & (seg >= halfway))
+    def _():
         greet(last - seg, band)
-        greet(last - seg, other)
 
     for m in range(batches):
 
-        @pl.when((seg != last) | (band != HALVES * m + own_half))
-        def _():
-            greet(last, HALVES * m + own_half)
+        @pl.when((seg != tail) | (band != HALVES * m + own_half))
+        def _():
+            greet(tail, HALVES * m + own_half)
 
     def one_if(condition):
         return jnp.where(condition, 1, 0).astype(jnp.int32)
@@ -126,10 +142,11 @@
     def pix_sends(worker):
         return (seg == 0) & (pix_chunk(worker) < chunks) & (band != worker)
 
-    expected = one_if(works & (seg < last)) * 2 + one_if(works & (seg < halfway - 1)) * 2
+    expected = one_if(works & (seg < tail)) * 2 + one_if(works & (seg < halfway - 2)) * 2
+    expected += one_if(feeds) + one_if(feeds & (seg < halfway))
     for worker in range(workers):
         expected += one_if(pix_sends(worker))
-    expected += one_if(works & (seg == last)) * (
+    expected += one_if(works & (seg == tail)) * (
         segments * half_bands - one_if(own_half == lower)
     )
 
@@ -160,18 +177,56 @@
             pix_ref.at[micro], pix_buf.at[own_chunk], pix_recv.at[own_chunk]
         ).start()
 
-    mirror_copy = pltpu.make_async_remote_copy(
-        src_ref=join_ref,
-        dst_ref=mirror_join,
-        send_sem=mirror_send,
-        recv_sem=mirror_recv,
-        device_id=(last - seg, band),
+    def feed_copy(layer, dy):
+        return pltpu.make_async_remote_copy(
+            src_ref=conv_ref.at[layer, dy],
+            dst_ref=weight_buf.at[layers + layer, dy + lower * (2 - 2 * dy)],
+            send_sem=feed_send.at[layer, dy],
+            recv_sem=feed_recv.at[layer, dy],
+            device_id=(seg - 1, band),
+            device_id_type=MESH,
+        )
+
+    def join_send(slot, to_seg, buffer, at):
+        return pltpu.make_async_remote_copy(
+            src_ref=join_ref,
+            dst_ref=buffer.at[at],
+            send_sem=mirror_send.at[slot],
+            recv_sem=mirror_recv.at[slot],
+            device_id=(to_seg, band),
+            device_id_type=MESH,
+        )
+
+    second_own = join_send(0, seg - 1, own_join, 1)
+    first_mirror = join_send(1, last - seg, mirror_join, 0)
+    second_mirror = join_send(2, tail - seg, mirror_join, 1)
+
+    @pl.when(feeds)
+    def _():
+        for layer in range(layers):
+            for dy in range(3):
+                feed_copy(layer, dy).start()
+
+    @pl.when(feeds & (seg >= halfway))
+    def _():
+        second_own.start()
+
+    @pl.when(feeds & (seg < halfway))
+    def _():
+        first_mirror.start()
+
+    @pl.when(works & (seg < halfway))
+    def _():
+        second_mirror.start()
+
+    early_copy = pltpu.make_async_remote_copy(
+        src_ref=early_out,
+        dst_ref=early_skip,
+        send_sem=early_send,
+        recv_sem=early_recv,
+        device_id=(tail - seg, band),
         device_id_type=MESH,
     )
-
-    @pl.when(works & (seg < halfway))
-    def _():
-        mirror_copy.start()
 
     def hop_copies(buffer, to_seg, send, recv):
         return (
@@ -193,8 +248,8 @@
             ),
         )
 
-    next_copies = hop_copies(in_buf, seg + 1, in_send, in_recv)
-    skip_copies = hop_copies(skip_buf, last - seg, skip_send, skip_recv)
+    next_copies = hop_copies(in_buf, seg + 2, in_send, in_recv)
+    skip_copies = hop_copies(skip_buf, tail - seg, skip_send, skip_recv)
 
     def fin_copy(g, k):
         return pltpu.make_async_remote_copy(
@@ -211,7 +266,7 @@
 
     @pl.when(works)
     def _():
-        @pl.when(seg == last)
+        @pl.when(seg == tail)
         def _():
             block_rows = fin_src.shape[1]
             at = lax.broadcasted_iota(jnp.int32, (block_rows, own_px), 0)
@@ -231,8 +286,7 @@
                     ).astype(jnp.bfloat16)
 
         hid[...] = jnp.zeros_like(hid)
-        span = 3 * channels
-        wide[pl.ds(0, columns)] = jnp.zeros((columns, span), jnp.bfloat16)
+        wide[pl.ds(0, columns)] = jnp.zeros((columns, 3 * channels), jnp.bfloat16)
         join_copy.wait()
 
         @pl.when(seg > 0)
@@ -242,13 +296,15 @@
 
         @pl.when(seg >= halfway)
         def _():
-            mirror_copy.wait_recv()
+            first_mirror.wait_recv()
+            second_mirror.wait_recv()
+            second_own.wait_recv()
 
         @pl.when(seg > halfway)
         def _():
             for copy in skip_copies:
                 copy.wait_recv()
-            skip_part[...] = dot(skip_buf[...], mirror_join[...])
+            skip_part[...] = dot(skip_buf[...], mirror_join[0])
 
         def take_input():
             @pl.when(seg == 0)
@@ -273,21 +329,32 @@
 
             @pl.when(seg == halfway)
             def _():
-                skip_part[...] = dot(in_buf[...], mirror_join[...])
+                skip_part[...] = dot(in_buf[...], mirror_join[0])
 
             @pl.when(seg >= halfway)
             def _():
-                hid[...] = (skip_part[...] + dot(in_buf[...], own_join[...])).astype(jnp.bfloat16)
-
-        keep = all_px - columns
-        at = lax.broadcasted_iota(jnp.int32, (all_px // columns, columns, channels), 1).reshape(
-            all_px, channels
-        )
-
-        first = -(-keep // (2 * columns)) * columns
-        blocks = ((0, first), (first, keep - first))
-
-        def step(index, carry):
+                hid[...] = (skip_part[...] + dot(in_buf[...], own_join[0])).astype(jnp.bfloat16)
+
+        def convolve(layer, count):
+            keep = count - columns
+            at = lax.broadcasted_iota(
+                jnp.int32, (count // columns, columns, channels), 1
+            ).reshape(count, channels)
+            scaled = unit(hid[pl.ds(0, count)].astype(jnp.float32))
+            left = jnp.where(at == 0, 0.0, pltpu.roll(scaled, 1, 0))
+            right = jnp.where(at == columns - 1, 0.0, pltpu.roll(scaled, count - 1, 0))
+            for dx, part in enumerate((left, scaled, right)):
+                wide[pl.ds(columns, count), pl.ds(dx * channels, channels)] = part.astype(
+                    jnp.bfloat16
+                )
+            total = dot(wide[pl.ds(0, keep)], weight_buf[layer, 0])
+            for dy in range(1, 3):
+                total += dot(wide[pl.ds(dy * columns, keep)], weight_buf[layer, dy])
+            hid[pl.ds(0, keep)] = (
+                hid[pl.ds(0, keep)].astype(jnp.float32) + jnp.maximum(total, 0.0)
+            ).astype(jnp.bfloat16)
+
+        def first_section(index, carry):
             @pl.when(index == 1)
             def _():
                 take_input()
@@ -301,26 +368,34 @@
                         conv_ref.at[layer, dy], weight_buf.at[layer, dy], weight_sem.at[layer, dy]
                     ).wait()
 
-            scaled = unit(hid[...].astype(jnp.float32))
-            left = jnp.where(at == 0, 0.0, pltpu.roll(scaled, 1, 0))
-            right = jnp.where(at == columns - 1, 0.0, pltpu.roll(scaled, all_px - 1, 0))
-            for dx, part in enumerate((left, scaled, right)):
-                wide[pl.ds(columns, all_px), pl.ds(dx * channels, channels)] = part.astype(
-                    jnp.bfloat16
-                )
-            for start, size in blocks:
-                total = dot(wide[pl.ds(start, size)], weight_buf[layer, 0])
-                for dy in range(1, 3):
-                    total += dot(wide[pl.ds(start + dy * columns, size)], weight_buf[layer, dy])
-                hid[pl.ds(start, size)] = (
-                    hid[pl.ds(start, size)].astype(jnp.float32) + jnp.maximum(total, 0.0)
-                ).astype(jnp.bfloat16)
+            convolve(layer, all_px)
             return carry
 
-        lax.fori_loop(one_if(seg == 0), layers + 1, step, 0)
+        lax.fori_loop(one_if(seg == 0), layers + 1, first_section, 0)
+        mid_px = early_out.shape[0]
+
+        @pl.when(seg < halfway)
+        def _():
+            early_out[...] = hid[pl.ds(0, mid_px)]
+            early_copy.start()
+
+        @pl.when(seg >= halfway)
+        def _():
+            early_copy.wait_recv()
+            hid[pl.ds(0, mid_px)] = (
+                dot(early_skip[...], mirror_join[1]) + dot(hid[pl.ds(0, mid_px)], own_join[1])
+            ).astype(jnp.bfloat16)
+
+        def second_section(layer, carry):
+            for dy in range(3):
+                feed_copy(layer, dy).wait_recv()
+            convolve(layers + layer, mid_px)
+            return carry
+
+        lax.fori_loop(0, layers, second_section, 0)
         hidden = hid[pl.ds(0, own_px)]
 
-        @pl.when(seg < last)
+        @pl.when(seg < tail)
         def _():
             for row in range(halo_px // columns):
                 start = own_px - (row + 1) * columns
@@ -329,19 +404,19 @@
             for copy in next_copies[::-1]:
                 copy.start()
 
-            @pl.when(seg < halfway - 1)
+            @pl.when(seg < halfway - 2)
             def _():
                 for copy in skip_copies:
                     copy.start()
 
-        @pl.when(seg == last)
+        @pl.when(seg == tail)
         def _():
             decoded = unit(hidden.astype(jnp.float32)).astype(jnp.bfloat16)
             sorting = place[...].reshape(-1, own_px)
             fin_src[...] = dot(sorting, decoded).astype(jnp.bfloat16).reshape(fin_src.shape)
             for g in range(segments):
                 for k in range(half_bands):
-                    if g < last:
+                    if g != tail:
                         fin_copy(g, k).start()
                     else:
                         here = chunk_band(k) == band
@@ -370,23 +445,38 @@
 
     @pl.when(works & (seg < halfway))
     def _():
-        mirror_copy.wait_send()
-
-    @pl.when(works & (seg < last))
+        second_mirror.wait_send()
+        early_copy.wait_send()
+
+    @pl.when(feeds)
+    def _():
+        for layer in range(layers):
+            for dy in range(3):
+                feed_copy(layer, dy).wait_send()
+
+    @pl.when(feeds & (seg >= halfway))
+    def _():
+        second_own.wait_send()
+
+    @pl.when(feeds & (seg < halfway))
+    def _():
+        first_mirror.wait_send()
+
+    @pl.when(works & (seg < tail))
     def _():
         for copy in next_copies:
             copy.wait_send()
 
-    @pl.when(works & (seg < halfway - 1))
+    @pl.when(works & (seg < halfway - 2))
     def _():
         for copy in skip_copies:
             copy.wait_send()
 
-    @pl.when(works & (seg == last))
+    @pl.when(works & (seg == tail))
     def _():
         for g in range(segments):
             for k in range(half_bands):
-                if g < last:
+                if g != tail:
                     fin_copy(g, k).wait_send()
                 else:
 
@@ -399,9 +489,10 @@
     batches, band_rows, columns, channels = pixels.shape
     layers = conv_weight.shape[1]
     own_rows = band_rows * bands // HALVES
-    rows = own_rows + layers
+    rows = own_rows + 2 * layers
     chunks = -(-rows // band_rows)
-    own_px, halo_px, all_px = own_rows * columns, layers * columns, rows * columns
+    own_px, halo_px, all_px = own_rows * columns, 2 * layers * columns, rows * columns
+    mid_px = (own_rows + layers) * columns
     share = columns // segments
     piece = band_rows * share
     block_rows = -(-piece // 16) * 16
@@ -420,9 +511,11 @@
             pltpu.VMEM((chunks, band_rows, columns, channels), kept),
             pltpu.VMEM((all_px, channels), kept),
             pltpu.VMEM((all_px, channels), kept),
-            pltpu.VMEM((layers, 3, 3 * channels, channels), kept),
-            pltpu.VMEM((channels, channels), kept),
-            pltpu.VMEM((channels, channels), kept),
+            pltpu.VMEM((mid_px, channels), kept),
+            pltpu.VMEM((mid_px, channels), kept),
+            pltpu.VMEM((2 * layers, 3, 3 * channels, channels), kept),
+            pltpu.VMEM((2, channels, channels), kept),
+            pltpu.VMEM((2, channels, channels), kept),
             pltpu.VMEM((all_px, channels), jnp.float32),
             pltpu.VMEM((all_px, channels), kept),
             pltpu.VMEM((all_px + columns, 3 * channels), kept),
@@ -439,6 +532,10 @@
             dma((2,)),
             dma((2,)),
             dma((2,)),
+            dma((3,)),
+            dma((3,)),
+            dma((layers, 3)),
+            dma((layers, 3)),
             dma,
             dma,
             dma((blocks,)),

time: 55.8 us -> 47.4 us (0.85)
  Pallas kernels: 54.2 us -> 45.9 us
    pallas_call x1, Pallas kernels: 54.2 us -> 45.9 us  [shards(): pl.pallas_call(functools.partial(kernel, segments, bands), out_shape=jax....]
where the time goes in v7:
time: 47.4 us; the launch traced here: 47.2 us
  Pallas kernels  45.9 us (97%)
  local copies, waits for them, and re-layouts  1.31 us (3%)
    pallas_call x1, Pallas kernels, shards(): pl.pallas_call(functools.partial(kernel, segments, bands), out_shape=jax....  45.9 us
    reshape x1, local copies, waits for them, and re-layouts, shards(): return result.reshape(batches, band_rows, share, channels)  1.31 us

profile of v7, /device:TPU:0, one launch (start us, length us, event | category | flops | bytes accessed | tf_op | source)
XLA Modules:
  0.0 47.2 jit_solution(10569216810710626238)
XLA Ops:
  0.0 45.9 %shard_map.37 = bf16[2,8,256]{2,1,0:T(8,128)(2,1)} custom-call(bf16[2,4,16,256]{3,2,1,0:T(8,128)(2,1)} %pix_ref.1, bf16[4,3,768,256]{3,2,1,0:T(8,128)(2,1)} %bitcast.2, bf16[256,256]{1,0:T(8,128)(2,1)} %bitcast.3), custom_call_target="tpu_custom_call" | custom-call | tf_op jit(solution)/shard_map/pallas_call | solution.py:505
  45.9 1.3 %reshape.11 = bf16[2,4,2,256]{3,2,1,0:T(2,128)(2,1)} reshape(bf16[2,8,256]{2,1,0:T(8,128)(2,1)} %shard_map.37) | data formatting | bytes 16384 | tf_op jit(solution)/shard_map/reshape | solution.py:546

commit v8 on v7

--- a/solution.py
+++ b/solution.py
@@ -354,45 +354,56 @@
                 hid[pl.ds(0, keep)].astype(jnp.float32) + jnp.maximum(total, 0.0)
             ).astype(jnp.bfloat16)
 
-        def first_section(index, carry):
-            @pl.when(index == 1)
+        mid_px = early_out.shape[0]
+
+        def both_sections(turn, carry):
+            real = turn == 1
+            count = jnp.where(real, layers, 1)
+
+            @pl.when(real)
             def _():
                 take_input()
 
-            layer = jnp.maximum(index - 1, 0)
-
-            @pl.when(seg == 0)
-            def _():
-                for dy in range(3):
-                    pltpu.make_async_copy(
-                        conv_ref.at[layer, dy], weight_buf.at[layer, dy], weight_sem.at[layer, dy]
-                    ).wait()
-
-            convolve(layer, all_px)
+            def first_section(layer, inner):
+                @pl.when(seg == 0)
+                def _():
+                    for dy in range(3):
+                        pltpu.make_async_copy(
+                            conv_ref.at[layer, dy],
+                            weight_buf.at[layer, dy],
+                            weight_sem.at[layer, dy],
+                        ).wait()
+
+                convolve(layer, all_px)
+                return inner
+
+            lax.fori_loop(0, count, first_section, 0)
+
+            @pl.when(real & (seg < halfway))
+            def _():
+                early_out[...] = hid[pl.ds(0, mid_px)]
+                early_copy.start()
+
+            @pl.when(real & (seg >= halfway))
+            def _():
+                early_copy.wait_recv()
+                hid[pl.ds(0, mid_px)] = (
+                    dot(early_skip[...], mirror_join[1]) + dot(hid[pl.ds(0, mid_px)], own_join[1])
+                ).astype(jnp.bfloat16)
+
+            def second_section(layer, inner):
+                @pl.when(real)
+                def _():
+                    for dy in range(3):
+                        feed_copy(layer, dy).wait_recv()
+
+                convolve(layer + jnp.where(real, layers, 0), mid_px)
+                return inner
+
+            lax.fori_loop(0, count, second_section, 0)
             return carry
 
-        lax.fori_loop(one_if(seg == 0), layers + 1, first_section, 0)
-        mid_px = early_out.shape[0]
-
-        @pl.when(seg < halfway)
-        def _():
-            early_out[...] = hid[pl.ds(0, mid_px)]
-            early_copy.start()
-
-        @pl.when(seg >= halfway)
-        def _():
-            early_copy.wait_recv()
-            hid[pl.ds(0, mid_px)] = (
-                dot(early_skip[...], mirror_join[1]) + dot(hid[pl.ds(0, mid_px)], own_join[1])
-            ).astype(jnp.bfloat16)
-
-        def second_section(layer, carry):
-            for dy in range(3):
-                feed_copy(layer, dy).wait_recv()
-            convolve(layers + layer, mid_px)
-            return carry
-
-        lax.fori_loop(0, layers, second_section, 0)
+        lax.fori_loop(one_if(seg == 0), 2, both_sections, 0)
         hidden = hid[pl.ds(0, own_px)]
 
         @pl.when(seg < tail)

time: 47.4 us -> 47.3 us (level)
  no operation moved by 1% of the time
where the time goes in v8:
time: 47.3 us; the launch traced here: 47.1 us
  Pallas kernels  45.8 us (97%)
  local copies, waits for them, and re-layouts  1.31 us (3%)
    pallas_call x1, Pallas kernels, shards(): pl.pallas_call(functools.partial(kernel, segments, bands), out_shape=jax....  45.8 us
    reshape x1, local copies, waits for them, and re-layouts, shards(): return result.reshape(batches, band_rows, share, channels)  1.31 us

profile of v8, /device:TPU:0, one launch (start us, length us, event | category | flops | bytes accessed | tf_op | source)
XLA Modules:
  0.0 47.1 jit_solution(8651745226434492214)
XLA Ops:
  0.0 45.8 %shard_map.37 = bf16[2,8,256]{2,1,0:T(8,128)(2,1)} custom-call(bf16[2,4,16,256]{3,2,1,0:T(8,128)(2,1)} %pix_ref.1, bf16[4,3,768,256]{3,2,1,0:T(8,128)(2,1)} %bitcast.2, bf16[256,256]{1,0:T(8,128)(2,1)} %bitcast.3), custom_call_target="tpu_custom_call" | custom-call | tf_op jit(solution)/shard_map/pallas_call | solution.py:516
  45.8 1.3 %reshape.11 = bf16[2,4,2,256]{3,2,1,0:T(2,128)(2,1)} reshape(bf16[2,8,256]{2,1,0:T(8,128)(2,1)} %shard_map.37) | data formatting | bytes 16384 | tf_op jit(solution)/shard_map/reshape | solution.py:557

commit v9 on v7

--- a/solution.py
+++ b/solution.py
@@ -285,14 +285,11 @@
                         inside & (pixel == wanted), 1.0, 0.0
                     ).astype(jnp.bfloat16)
 
-        hid[...] = jnp.zeros_like(hid)
         wide[pl.ds(0, columns)] = jnp.zeros((columns, 3 * channels), jnp.bfloat16)
         join_copy.wait()
 
-        @pl.when(seg > 0)
-        def _():
-            for copy in weight_copies:
-                copy.wait()
+        for copy in weight_copies:
+            copy.wait()
 
         @pl.when(seg >= halfway)
         def _():
@@ -354,25 +351,11 @@
                 hid[pl.ds(0, keep)].astype(jnp.float32) + jnp.maximum(total, 0.0)
             ).astype(jnp.bfloat16)
 
-        def first_section(index, carry):
-            @pl.when(index == 1)
-            def _():
-                take_input()
-
-            layer = jnp.maximum(index - 1, 0)
-
-            @pl.when(seg == 0)
-            def _():
-                for dy in range(3):
-                    pltpu.make_async_copy(
-                        conv_ref.at[layer, dy], weight_buf.at[layer, dy], weight_sem.at[layer, dy]
-                    ).wait()
-
-            convolve(layer, all_px)
-            return carry
-
-        lax.fori_loop(one_if(seg == 0), layers + 1, first_section, 0)
         mid_px = early_out.shape[0]
+
+        take_input()
+        for layer in range(layers):
+            convolve(layer, all_px - layer * columns)
 
         @pl.when(seg < halfway)
         def _():
@@ -386,13 +369,10 @@
                 dot(early_skip[...], mirror_join[1]) + dot(hid[pl.ds(0, mid_px)], own_join[1])
             ).astype(jnp.bfloat16)
 
-        def second_section(layer, carry):
+        for layer in range(layers):
             for dy in range(3):
                 feed_copy(layer, dy).wait_recv()
-            convolve(layers + layer, mid_px)
-            return carry
-
-        lax.fori_loop(0, layers, second_section, 0)
+            convolve(layers + layer, mid_px - layer * columns)
         hidden = hid[pl.ds(0, own_px)]
 
         @pl.when(seg < tail)

time: 47.4 us -> 52.5 us (1.11)
  Pallas kernels: 45.9 us -> 50.9 us
    pallas_call x1, Pallas kernels: 45.9 us -> 50.9 us  [shards(): pl.pallas_call(functools.partial(kernel, segments, bands), out_shape=jax....]
where the time goes in v9:
time: 52.5 us; the launch traced here: 52.2 us
  Pallas kernels  50.9 us (97%)
  local copies, waits for them, and re-layouts  1.31 us (2%)
    pallas_call x1, Pallas kernels, shards(): pl.pallas_call(functools.partial(kernel, segments, bands), out_shape=jax....  50.9 us
    reshape x1, local copies, waits for them, and re-layouts, shards(): return result.reshape(batches, band_rows, share, channels)  1.31 us

profile of v9, /device:TPU:0, one launch (start us, length us, event | category | flops | bytes accessed | tf_op | source)
XLA Modules:
  0.0 52.2 jit_solution(15698605819380672881)
XLA Ops:
  0.0 50.9 %shard_map.37 = bf16[2,8,256]{2,1,0:T(8,128)(2,1)} custom-call(bf16[2,4,16,256]{3,2,1,0:T(8,128)(2,1)} %pix_ref.1, bf16[4,3,768,256]{3,2,1,0:T(8,128)(2,1)} %bitcast.2, bf16[256,256]{1,0:T(8,128)(2,1)} %bitcast.3), custom_call_target="tpu_custom_call" | custom-call | tf_op jit(solution)/shard_map/pallas_call | solution.py:485
  50.9 1.3 %reshape.11 = bf16[2,4,2,256]{3,2,1,0:T(2,128)(2,1)} reshape(bf16[2,8,256]{2,1,0:T(8,128)(2,1)} %shard_map.37) | data formatting | bytes 16384 | tf_op jit(solution)/shard_map/reshape | solution.py:526

commit v10 on v8

--- a/solution.py
+++ b/solution.py
@@ -365,7 +365,7 @@
                 take_input()
 
             def first_section(layer, inner):
-                @pl.when(seg == 0)
+                @pl.when((seg == 0) & (real == (layer > 0)))
                 def _():
                     for dy in range(3):
                         pltpu.make_async_copy(
@@ -403,7 +403,7 @@
             lax.fori_loop(0, count, second_section, 0)
             return carry
 
-        lax.fori_loop(one_if(seg == 0), 2, both_sections, 0)
+        lax.fori_loop(0, 2, both_sections, 0)
         hidden = hid[pl.ds(0, own_px)]
 
         @pl.when(seg < tail)

time: 47.3 us -> 47.4 us (level)
  no operation moved by 1% of the time
where the time goes in v10:
time: 47.4 us; the launch traced here: 47.2 us
  Pallas kernels  45.8 us (97%)
  local copies, waits for them, and re-layouts  1.31 us (3%)
    pallas_call x1, Pallas kernels, shards(): pl.pallas_call(functools.partial(kernel, segments, bands), out_shape=jax....  45.8 us
    reshape x1, local copies, waits for them, and re-layouts, shards(): return result.reshape(batches, band_rows, share, channels)  1.31 us

profile of v10, /device:TPU:0, one launch (start us, length us, event | category | flops | bytes accessed | tf_op | source)
XLA Modules:
  0.0 47.2 jit_solution(15490700921619010788)
XLA Ops:
  0.0 45.8 %shard_map.37 = bf16[2,8,256]{2,1,0:T(8,128)(2,1)} custom-call(bf16[2,4,16,256]{3,2,1,0:T(8,128)(2,1)} %pix_ref.1, bf16[4,3,768,256]{3,2,1,0:T(8,128)(2,1)} %bitcast.2, bf16[256,256]{1,0:T(8,128)(2,1)} %bitcast.3), custom_call_target="tpu_custom_call" | custom-call | tf_op jit(solution)/shard_map/pallas_call | solution.py:516
  45.8 1.3 %reshape.11 = bf16[2,4,2,256]{3,2,1,0:T(2,128)(2,1)} reshape(bf16[2,8,256]{2,1,0:T(8,128)(2,1)} %shard_map.37) | data formatting | bytes 16384 | tf_op jit(solution)/shard_map/reshape | solution.py:557

commit v11 on v8

--- a/solution.py
+++ b/solution.py
@@ -231,7 +231,7 @@
     def hop_copies(buffer, to_seg, send, recv):
         return (
             pltpu.make_async_remote_copy(
-                src_ref=own_out,
+                src_ref=hid.at[pl.ds(0, own_px)],
                 dst_ref=buffer.at[pl.ds(0, own_px)],
                 send_sem=send.at[0],
                 recv_sem=recv.at[0],
@@ -411,7 +411,6 @@
             for row in range(halo_px // columns):
                 start = own_px - (row + 1) * columns
                 halo_out[pl.ds(row * columns, columns)] = hidden[start : start + columns]
-            own_out[...] = hidden
             for copy in next_copies[::-1]:
                 copy.start()
 

time: 47.3 us -> 47.3 us (level)
  no operation moved by 1% of the time
where the time goes in v11:
time: 47.3 us; the launch traced here: 47.1 us
  Pallas kernels  45.8 us (97%)
  local copies, waits for them, and re-layouts  1.31 us (3%)
    pallas_call x1, Pallas kernels, shards(): pl.pallas_call(functools.partial(kernel, segments, bands), out_shape=jax....  45.8 us
    reshape x1, local copies, waits for them, and re-layouts, shards(): return result.reshape(batches, band_rows, share, channels)  1.31 us

profile of v11, /device:TPU:0, one launch (start us, length us, event | category | flops | bytes accessed | tf_op | source)
XLA Modules:
  0.0 47.1 jit_solution(12553228902271519417)
XLA Ops:
  0.0 45.8 %shard_map.37 = bf16[2,8,256]{2,1,0:T(8,128)(2,1)} custom-call(bf16[2,4,16,256]{3,2,1,0:T(8,128)(2,1)} %pix_ref.1, bf16[4,3,768,256]{3,2,1,0:T(8,128)(2,1)} %bitcast.2, bf16[256,256]{1,0:T(8,128)(2,1)} %bitcast.3), custom_call_target="tpu_custom_call" | custom-call | tf_op jit(solution)/shard_map/pallas_call | solution.py:515
  45.8 1.3 %reshape.11 = bf16[2,4,2,256]{3,2,1,0:T(2,128)(2,1)} reshape(bf16[2,8,256]{2,1,0:T(8,128)(2,1)} %shard_map.37) | data formatting | bytes 16384 | tf_op jit(solution)/shard_map/reshape | solution.py:556
